TPU v7x, 32 devices: a whole 2x2x4 slice. The times are simulated.
32 devices in a mesh: grp: 4 (over y, x), tok: 8 (over z, core).
Axes of the slice: x: 2, y: 2, z: 4, core: 2. Of those that a mesh axis runs over, the one named last changes fastest.
Arguments:
- tokens: float32 [32768, 768], P(('grp', 'tok')), may hold values from -6 to 6
- cotangent: float32 [32768, 768], P(('grp', 'tok')), may hold values from -6 to 6
- crop_lengths: int32 [32, 10], P(('grp', 'tok')), may hold values from 54 to 261, as said below
- master: float32 [7088640], P('tok')
- first_moment: float32 [4, 7088640], P('grp', 'tok')
- second_moment: float32 [4, 7088640], P('grp', 'tok')
- outer_momentum: float32 [7088640], P('tok'), may hold values from -0.4375 to 0.4375
Outputs:
- block_output: float32 [32768, 768], P(('grp', 'tok'))
- input_grad: float32 [32768, 768], P(('grp', 'tok'))
- clip_norm: float32 [4], P('grp')
- vector_grads: float32 [4, 10752], P('grp', 'tok')
- first_moment_new: float32 [4, 7088640], P('grp', 'tok')
- second_moment_new: float32 [4, 7088640], P('grp', 'tok')
- mean_difference: float32 [7088640], P('tok')
- outer_momentum_new: float32 [7088640], P('tok')
- new_weights: float32 [7088640], P('tok')
Inputs may be any that keep to these rules, and one draw needn't show every extreme that they name: `crop_lengths`: each row holds, for each of its 1 images, 261 * 2 times and 54 * 8 times, in a drawn order.
All inputs are finite; a program needn't handle non-finite values.
Results may differ from a plain program's by a relative error of at most 0.012.
The roundings to bfloat16 on the way count: a program that leaves them out, or rounds other values in their place, can miss the bound.
Values may be sent and summed in bfloat16 or wider, within the bound.
A program may use at most 256 MiB of HBM per device.

v0:
```python
import jax
import jax.numpy as jnp
from jax import lax
from jax.experimental import pallas as pl
from jax.experimental.pallas import tpu as pltpu
from jax.sharding import PartitionSpec as P

D = 768
MLP = 3072
HEADS = 12
HEAD_DIM = 64
ROWS = D // 8
ANY = pl.BlockSpec(memory_space=pl.ANY)
DMA = pltpu.SemaphoreType.DMA
MESH_ID = pl.DeviceIdType.MESH
NZ = 4
F32, BF16 = jnp.float32, jnp.bfloat16


def place():
    g = lax.axis_index("grp")
    t = lax.axis_index("tok")
    z, c = lax.div(t, 2), lax.rem(t, 2)
    gx = g + 1 - 2 * lax.rem(g, 2)
    gy = g + 2 - 4 * lax.div(g, 2)
    return g, t, z, c, gx, gy


def greet(targets, count):
    barrier = pltpu.get_barrier_semaphore()
    for target in targets:
        pl.semaphore_signal(barrier, inc=1, device_id=target, device_id_type=MESH_ID)
    pl.semaphore_wait(barrier, count)


def remote(src, dst, send, recv, target):
    return pltpu.make_async_remote_copy(
        src_ref=src, dst_ref=dst, send_sem=send, recv_sem=recv,
        device_id=target, device_id_type=MESH_ID,
    )


clip_limit = 3.0
beta_first = 0.9
beta_second = 0.999
adam_epsilon = 1e-08
weight_decay = 0.04
adam_count = 10.0
base_rate = 0.075
rate_scale = 0.9**6
outer_rate = 0.7
outer_beta = 0.9
norm_epsilon = 1e-06


def member_extents():
    return [(D, 3 * D), (D, D), (D, MLP), (MLP, D)] + [(D,)] * 8 + [(MLP,), (D,), (D,)]


def member_sizes():
    sizes_list = []
    for extent in member_extents():
        length = 1
        for member in extent:
            length = length * member
        sizes_list.append(length)
    return sizes_list


def split_params(flat_params, owners):
    table = flat_params.reshape(owners, -1)
    members = []
    offset = 0
    for extent, length in zip(member_extents(), member_sizes()):
        width = length // owners
        members.append(table[:, offset : offset + width].reshape(extent))
        offset = offset + width
    return members


def join_table(members, owners):
    return jnp.concatenate([member.reshape(owners, -1) for member in members], axis=1)


def layer_norm(values, norm_gain, norm_shift):
    center = values - jnp.mean(values, axis=-1, keepdims=True)
    spread = jnp.mean(center * center, axis=-1, keepdims=True)
    return center * lax.rsqrt(spread + norm_epsilon) * norm_gain + norm_shift


def pack_layout(lengths_row, row_count):
    ends_at = jnp.cumsum(lengths_row)
    position = jnp.arange(row_count, dtype=jnp.int32)
    segment = jnp.sum((position[:, None] >= ends_at[None, :]).astype(jnp.int32), axis=1)
    validity = (position < ends_at[-1]).astype(jnp.float32)
    return (segment, validity)


def cross_rows(left_side, right_side):
    return lax.dot_general(
        left_side, right_side, (((0,), (0,)), ((), ())), preferred_element_type=jnp.float32
    )


def times_transposed(left_side, right_side):
    return lax.dot_general(
        left_side, right_side, (((1,), (1,)), ((), ())), preferred_element_type=jnp.float32
    )


def on_device(tokens, cotangent, crop_lengths, master, first_moment, second_moment, outer_momentum):
    row_count = tokens.shape[0]
    pair_count = HEADS // 2
    score_scale = HEAD_DIM ** (-0.5)
    owners = lax.axis_size("tok")
    segment, validity = pack_layout(crop_lengths[0], row_count)
    allowed = segment[:, None] == segment[None, :]
    master_low = master.astype(jnp.bfloat16)
    gathered = split_params(lax.all_gather(master_low, "tok", axis=0, tiled=True), owners)
    w_qkv, w_proj, w_fc1, w_fc2 = gathered[:4]
    (
        gain_one,
        shift_one,
        query_bias,
        value_bias,
        proj_bias,
        scale_one,
        gain_two,
        shift_two,
        fc1_bias,
        fc2_bias,
        scale_two,
    ) = [member.astype(jnp.float32) for member in gathered[4:]]

    def to_pairs(block_cols):
        return jnp.moveaxis(block_cols.reshape(row_count, pair_count, 2 * HEAD_DIM), 1, 0)

    def from_pairs(paired):
        return jnp.moveaxis(paired, 0, 1).reshape(row_count, D)

    normed = layer_norm(tokens, gain_one, shift_one).astype(jnp.bfloat16)
    qkv_bias = jnp.concatenate([query_bias, jnp.zeros_like(query_bias), value_bias])
    projected = (jnp.dot(normed, w_qkv, preferred_element_type=jnp.float32) + qkv_bias).astype(
        jnp.bfloat16
    )
    query_pairs = to_pairs(projected[:, :D])
    key_pairs = to_pairs(projected[:, D : 2 * D])
    value_pairs = to_pairs(projected[:, 2 * D :])

    def forward_pair(pair_item):
        queries, keys_pair, values_pair = [
            member.reshape(row_count, 2, HEAD_DIM) for member in pair_item
        ]
        raw_scores = jnp.einsum(
            "qhd,khd->hqk", queries, keys_pair, preferred_element_type=jnp.float32
        )
        scores = jnp.where(allowed[None], raw_scores * score_scale, -1e30)
        largest = jnp.max(scores, axis=-1, keepdims=True)
        weights_exp = jnp.exp(scores - largest)
        totals = jnp.sum(weights_exp, axis=-1, keepdims=True)
        weights_low = (weights_exp / totals).astype(jnp.bfloat16)
        attended_pair = jnp.einsum(
            "hqk,khd->qhd", weights_low, values_pair, preferred_element_type=jnp.float32
        )
        return (attended_pair.reshape(row_count, 2 * HEAD_DIM), (largest + jnp.log(totals))[..., 0])

    attended_pairs, log_totals = lax.map(forward_pair, (query_pairs, key_pairs, value_pairs))
    attended = from_pairs(attended_pairs).astype(jnp.bfloat16)
    branch_one = jnp.dot(attended, w_proj, preferred_element_type=jnp.float32) + proj_bias
    middle = tokens + scale_one * branch_one
    normed_two = layer_norm(middle, gain_two, shift_two).astype(jnp.bfloat16)
    hidden_pre = jnp.dot(normed_two, w_fc1, preferred_element_type=jnp.float32) + fc1_bias
    hidden = jax.nn.gelu(hidden_pre, approximate=False).astype(jnp.bfloat16)
    branch_two = jnp.dot(hidden, w_fc2, preferred_element_type=jnp.float32) + fc2_bias
    block_output = middle + scale_two * branch_two
    back_out = cotangent * validity[:, None]
    grad_branch_two = (scale_two * back_out).astype(jnp.bfloat16)
    grad_scale_two = jnp.sum(back_out * branch_two, axis=0)
    grad_fc2_bias = jnp.sum(grad_branch_two.astype(jnp.float32), axis=0)
    grad_w_fc2 = cross_rows(hidden, grad_branch_two)
    grad_hidden = times_transposed(grad_branch_two, w_fc2)
    gelu_pull = jax.vjp(lambda values: jax.nn.gelu(values, approximate=False), hidden_pre)[1]
    grad_pre = gelu_pull(grad_hidden)[0].astype(jnp.bfloat16)
    grad_fc1_bias = jnp.sum(grad_pre.astype(jnp.float32), axis=0)
    grad_w_fc1 = cross_rows(normed_two, grad_pre)
    grad_normed_two = times_transposed(grad_pre, w_fc1)
    norm_pull = jax.vjp(layer_norm, middle, gain_two, shift_two)[1]
    grad_middle_part, grad_gain_two, grad_shift_two = norm_pull(grad_normed_two)
    grad_middle = back_out + grad_middle_part
    grad_scale_one = jnp.sum(grad_middle * branch_one, axis=0)
    grad_branch_one = (scale_one * grad_middle).astype(jnp.bfloat16)
    grad_proj_bias = jnp.sum(grad_branch_one.astype(jnp.float32), axis=0)
    grad_w_proj = cross_rows(attended, grad_branch_one)
    grad_attended = times_transposed(grad_branch_one, w_proj).astype(jnp.bfloat16)

    def backward_pair(pair_item):
        queries, keys_pair, values_pair, grad_pair = [
            member.reshape(row_count, 2, HEAD_DIM) for member in pair_item[:4]
        ]
        log_total = pair_item[4]
        raw_scores = jnp.einsum(
            "qhd,khd->hqk", queries, keys_pair, preferred_element_type=jnp.float32
        )
        scores = jnp.where(allowed[None], raw_scores * score_scale, -1e30)
        weights_soft = jnp.exp(scores - log_total[..., None])
        grad_values = jnp.einsum(
            "hqk,qhd->khd",
            weights_soft.astype(jnp.bfloat16),
            grad_pair,
            preferred_element_type=jnp.float32,
        )
        grad_weights = jnp.einsum(
            "qhd,khd->hqk", grad_pair, values_pair, preferred_element_type=jnp.float32
        )
        row_dot = jnp.sum(weights_soft * grad_weights, axis=-1, keepdims=True)
        grad_scores = (weights_soft * (grad_weights - row_dot)).astype(jnp.bfloat16)
        grad_queries = (
            jnp.einsum("hqk,khd->qhd", grad_scores, keys_pair, preferred_element_type=jnp.float32)
            * score_scale
        )
        grad_keys = (
            jnp.einsum("hqk,qhd->khd", grad_scores, queries, preferred_element_type=jnp.float32)
            * score_scale
        )
        return (
            grad_queries.reshape(row_count, 2 * HEAD_DIM),
            grad_keys.reshape(row_count, 2 * HEAD_DIM),
            grad_values.reshape(row_count, 2 * HEAD_DIM),
        )

    grad_q_pairs, grad_k_pairs, grad_v_pairs = lax.map(
        backward_pair, (query_pairs, key_pairs, value_pairs, to_pairs(grad_attended), log_totals)
    )
    grad_projected = jnp.concatenate(
        [from_pairs(grad_q_pairs), from_pairs(grad_k_pairs), from_pairs(grad_v_pairs)], axis=1
    ).astype(jnp.bfloat16)
    grad_query_bias = jnp.sum(grad_projected[:, :D].astype(jnp.float32), axis=0)
    grad_value_bias = jnp.sum(grad_projected[:, 2 * D :].astype(jnp.float32), axis=0)
    grad_w_qkv = cross_rows(normed, grad_projected)
    grad_normed = times_transposed(grad_projected, w_qkv)
    first_pull = jax.vjp(layer_norm, tokens, gain_one, shift_one)[1]
    grad_tokens_part, grad_gain_one, grad_shift_one = first_pull(grad_normed)
    input_grad = grad_middle + grad_tokens_part
    all_members = [
        grad_w_qkv,
        grad_w_proj,
        grad_w_fc1,
        grad_w_fc2,
        grad_gain_one,
        grad_shift_one,
        grad_query_bias,
        grad_value_bias,
        grad_proj_bias,
        grad_scale_one,
        grad_gain_two,
        grad_shift_two,
        grad_fc1_bias,
        grad_fc2_bias,
        grad_scale_two,
    ]
    received = lax.all_to_all(
        join_table(all_members, owners).astype(jnp.bfloat16),
        "tok",
        split_axis=0,
        concat_axis=0,
        tiled=True,
    ).astype(jnp.float32)
    summed = jnp.sum(received, axis=0)
    matrix_width = (4 * D * D + 2 * D * MLP) // owners
    vector_part = summed[matrix_width:] / (owners * row_count) ** 0.5
    square_total = lax.psum(jnp.sum(summed * summed), "tok")
    norm_value = jnp.sqrt(square_total)
    clipped = summed * (clip_limit / (norm_value + 1e-06))
    moment_one = beta_first * first_moment[0] + (1.0 - beta_first) * clipped
    moment_two = beta_second * second_moment[0] + (1.0 - beta_second) * clipped * clipped
    corrected_one = moment_one / (1.0 - beta_first**adam_count)
    corrected_two = moment_two / (1.0 - beta_second**adam_count)
    shard_size = master.shape[0]
    local_index = jnp.arange(shard_size, dtype=jnp.int32)
    decay_mask = (local_index < matrix_width).astype(jnp.float32)
    step_rate = base_rate * rate_scale
    updated = master - step_rate * (
        corrected_one / (jnp.sqrt(corrected_two) + adam_epsilon)
        + weight_decay * decay_mask * master
    )
    mean_difference = lax.psum((master - updated).astype(jnp.bfloat16), "grp").astype(
        jnp.float32
    ) / lax.axis_size("grp")
    outer_new = outer_beta * outer_momentum + mean_difference
    new_weights = master - outer_rate * (mean_difference + outer_beta * outer_new)
    return (
        block_output,
        input_grad,
        norm_value.reshape(1),
        vector_part[None],
        moment_one[None],
        moment_two[None],
        mean_difference,
        outer_new,
        new_weights,
    )


def rows_at(ref, start, count):
    return ref.at[pl.ds(pl.multiple_of(start, 16), count), :]

TILE = 256


def nn(a, b):
    return lax.dot_general(a, b, (((1,), (0,)), ((), ())), preferred_element_type=F32)


def nt(a, b):
    return lax.dot_general(a, b, (((1,), (1,)), ((), ())), preferred_element_type=F32)


def tn(a, b):
    return lax.dot_general(a, b, (((0,), (0,)), ((), ())), preferred_element_type=F32)


def normalize(values):
    center = values - jnp.mean(values, axis=-1, keepdims=True)
    spread = jnp.mean(center * center, axis=-1, keepdims=True)
    inverse = lax.rsqrt(spread + norm_epsilon)
    return center * inverse, inverse


def norm_pull(grad, normal, inverse, gain):
    scaled = grad * gain
    return inverse * (
        scaled
        - jnp.mean(scaled, axis=-1, keepdims=True)
        - normal * jnp.mean(scaled * normal, axis=-1, keepdims=True)
    )


def gelu_and_slope(x):
    phi = 0.5 * (1.0 + lax.erf(x * 0.7071067811865476))
    return x * phi, phi + x * jnp.exp(-0.5 * x * x) * 0.3989422804014327


def col_sum(x):
    return jnp.sum(x, axis=0, keepdims=True)


QT = 256
LONG, SHORT = 261, 54
TILES = (
    (0, 272, 0, 384, 0, 261),
    (256, 272, 256, 384, 261, 522),
    (512, 288, 512, 384, 522, 792),
    (784, 240, 768, 256, 792, 1024),
)


def find_places(lens, line, column):
    crops = lens.shape[1]
    longs, shorts, begin = jnp.int32(0), jnp.int32(0), jnp.int32(0)
    at_line = lax.broadcasted_iota(jnp.int32, line.shape, 1)
    at_column = lax.broadcasted_iota(jnp.int32, column.shape, 0)
    new_line, new_column = at_line, at_column
    for j in range(crops):
        size = lens[0, j]
        is_long = (size == LONG).astype(jnp.int32)
        place_at = is_long * (longs * LONG) + (1 - is_long) * (2 * LONG + shorts * SHORT)
        shift = place_at - begin
        new_line = jnp.where((at_line >= begin) & (at_line < begin + size), at_line + shift, new_line)
        new_column = jnp.where((at_column >= begin) & (at_column < begin + size), at_column + shift, new_column)
        longs, shorts, begin = longs + is_long, shorts + 1 - is_long, begin + size
    line[...] = new_line
    column[...] = new_column


def to_places(line, first, count):
    rows = lax.broadcasted_iota(jnp.int32, (count, line.shape[1]), 0) + first
    return (rows == line[0:1, :]).astype(F32).astype(BF16)


def from_places(column, first, count):
    lanes = lax.broadcasted_iota(jnp.int32, (count, column.shape[0]), 1)
    return (lanes == column[pl.ds(first, count), 0:1]).astype(F32).astype(BF16)


def fill_bias(bias):
    def crop(at):
        found = jnp.zeros(at.shape, jnp.int32)
        for end in [LONG] + [2 * LONG + SHORT * j for j in range(9)]:
            found = found + (at >= end).astype(jnp.int32)
        return found

    for i, (row, rows, col, cols, low, high) in enumerate(TILES):
        at_row = lax.broadcasted_iota(jnp.int32, (rows, 1), 0) + row
        at_col = lax.broadcasted_iota(jnp.int32, (1, cols), 1) + col
        same = crop(at_row) == jnp.where((at_col >= low) & (at_col < high), crop(at_col), -1)
        bias[i, :rows, :cols] = jnp.where(same, 0.0, -1e30).astype(F32)


def head_part(block, h):
    lane = lax.broadcasted_iota(jnp.int32, (1, 128), 1)
    keep = lane < 64 if h == 0 else lane >= 64
    return jnp.where(keep, block, jnp.zeros_like(block))


def first_half(a, b):
    lane = lax.broadcasted_iota(jnp.int32, (1, 128), 1)
    return jnp.where(lane < 64, a, b)


def rows_from(tile, new, old):
    row, rows, low = tile[0], tile[1], tile[4]
    if row == low:
        return new
    return jnp.where(lax.broadcasted_iota(jnp.int32, (rows, 1), 0) + row >= low, new, old)


def norm_rows(tok, vec, normed):
    def tile(i, _):
        at = pl.ds(pl.multiple_of(i * QT, QT), QT)
        normal, _inverse = normalize(tok[at, :])
        normed[at, :] = (normal * vec[0:1, :] + vec[1:2, :]).astype(BF16)
        return 0
    lax.fori_loop(0, tok.shape[0] // QT, tile, 0)


def project_in(vec, wa, normed, proj):
    def block(i, _):
        at = pl.ds(pl.multiple_of(i * QT, QT), QT)
        proj[0, at, :] = (nn(normed[at, :], wa[0]) + vec[2:3, :]).astype(BF16)
        proj[1, at, :] = nn(normed[at, :], wa[1]).astype(BF16)
        proj[2, at, :] = (nn(normed[at, :], wa[2]) + vec[3:4, :]).astype(BF16)
        return 0
    lax.fori_loop(0, normed.shape[0] // QT, block, 0)


def move_rows(one_hot, src, dst):
    def block(i, _):
        first = pl.multiple_of(i * QT, QT)
        dst[pl.ds(first, QT), :] = nn(one_hot(first, QT), src[...]).astype(BF16)
        return 0
    lax.fori_loop(0, src.shape[0] // QT, block, 0)


def attend(p, proj, bias, att, lse):
    cols = pl.ds(pl.multiple_of(p * 128, 128), 128)
    lane = lax.broadcasted_iota(jnp.int32, (1, 128), 1)
    for i, tile in enumerate(TILES):
        row, rows, col, wide = tile[:4]
        at, keys = pl.ds(row, rows), pl.ds(col, wide)
        q = proj[0, at, cols] * jnp.asarray(0.125, BF16)
        k, v = proj[1, keys, cols], proj[2, keys, cols]
        outs = []
        logs = lse[at, :]
        for h in (0, 1):
            scores = nt(head_part(q, h), k) + bias[i, :rows, :wide]
            largest = jnp.max(scores, axis=-1, keepdims=True)
            weights = jnp.exp(scores - largest)
            total = jnp.sum(weights, axis=-1, keepdims=True)
            low = (weights * (1.0 / total)).astype(BF16)
            outs.append(nn(low, v))
            logs = jnp.where(lane == 2 * p + h, largest + jnp.log(total), logs)
        lse[at, :] = rows_from(tile, logs, lse[at, :])
        att[at, cols] = rows_from(tile, first_half(*outs), att[at, cols].astype(F32)).astype(BF16)


def attend_back(p, proj, gatt, bias, lse_t, dq):
    cols = pl.ds(pl.multiple_of(p * 128, 128), 128)
    dq[...] = jnp.zeros_like(dq)
    dks, dvs = [], []
    for i, tile in enumerate(TILES):
        row, rows, col, wide = tile[:4]
        at, queries = pl.ds(row, rows), pl.ds(col, wide)
        k, v = proj[1, at, cols], proj[2, at, cols]
        g = gatt[queries, cols]
        scaled = proj[0, queries, cols] * jnp.asarray(0.125, BF16)
        dk, dv, dqs = [], [], []
        for h in (0, 1):
            scores = nt(head_part(k, h), scaled) + bias[i, :rows, :wide]
            probs = jnp.exp(scores - lse_t[pl.ds(2 * p + h, 1), queries])
            grad = nt(head_part(v, h), g)
            dot = jnp.sum(probs * grad, axis=0, keepdims=True)
            low = (probs * (grad - dot)).astype(BF16)
            dv.append(nn(probs.astype(BF16), g))
            dk.append(nn(low, scaled))
            dqs.append(tn(low, k))
        dq[queries, :] += first_half(*dqs) * 0.125
        dks.append(first_half(*dk))
        dvs.append(first_half(*dv))
    for i, tile in enumerate(TILES):
        at = pl.ds(tile[0], tile[1])
        proj[1, at, cols] = rows_from(tile, dks[i], proj[1, at, cols].astype(F32)).astype(BF16)
        proj[2, at, cols] = rows_from(tile, dvs[i], proj[2, at, cols].astype(F32)).astype(BF16)
    proj[0, :, cols] = dq[...].astype(BF16)


def weight_grads(normed, gproj, gout):
    def block(q, _):
        def part(m, _):
            col = pl.ds(pl.multiple_of(m * 384, 128), 384)
            gout[:, q, :, col] = tn(normed[...], gproj[q, :, col]).astype(BF16).reshape(8, ROWS, 384)
            return 0
        return lax.fori_loop(0, 2, part, 0)
    lax.fori_loop(0, 3, block, 0)


def row_grads(column, wide, total, vec, wa, gproj, vg):

    def tile(i, _):
        first = pl.multiple_of(i * QT, QT)
        at = pl.ds(first, QT)
        back = from_places(column, first, QT)
        parts = [nn(back, gproj[j]).astype(BF16) for j in range(3)]
        grad = nt(parts[0], wa[0]) + nt(parts[1], wa[1]) + nt(parts[2], wa[2])
        normal, inverse = normalize(wide[at, :D])
        vg[0:1, :] += col_sum(grad * normal)
        vg[1:2, :] += col_sum(grad)
        vg[2:3, :] += col_sum(parts[0].astype(F32))
        vg[3:4, :] += col_sum(parts[2].astype(F32))
        total[at, :] = total[at, :] + norm_pull(grad, normal, inverse, vec[0:1, :])
        return 0
    lax.fori_loop(0, total.shape[0] // QT, tile, 0)


def convert_piece(w, lin, piece):
    if w == 2:
        for q in range(4):
            for m in range(6):
                piece[q, :, 128 * m : 128 * m + 128] = lin[pl.ds(4608 + 576 * q + m, ROWS, stride=6), :].astype(BF16)
        return
    for q in range(4):
        for m in range(6):
            if w == 1:
                at = pl.ds(2304 + 6 * q + m, ROWS, stride=24)
            elif q == 3:
                at = pl.ds(1728 + m, ROWS, stride=6)
            else:
                at = pl.ds(6 * q + m, ROWS, stride=18)
            piece[q, :, 128 * m : 128 * m + 128] = lin[at, :].astype(BF16)


def weight_strip(w, ref, t):
    if w == 2:
        return ref.at[t]
    return ref.at[:, pl.ds(pl.multiple_of(t * ROWS, 16), ROWS), :]


def weight_block(w, ref, t, q, half=None):
    lead, count = (0, ROWS) if half is None else (48 * half, 48)
    if w == 2:
        return ref.at[t, q, pl.ds(lead, count), :]
    return ref.at[q, pl.ds(pl.multiple_of(t * ROWS + lead, 16), count), :]


def front_kernel(
    lens, lin, pv, tok,
    wa, wb, wc, vec, fb1, normed, proj, att, lse_out,
    pieces, wv, wa_in, bias, line, column, att_in, lse,
    ls, zs, zr, xs, xr, ys, yr, ds, dr, cs, cr, vs, vr,
):
    g, t, z, c, gx, gy = place()
    fulls = (wa, wb, wc)
    peers = [lax.rem(t + k, 8) for k in range(1, 8)]
    barrier = pltpu.get_barrier_semaphore()
    for target in [(g, p) for p in peers] + [(gx, t), (gy, t)]:
        pl.semaphore_signal(barrier, inc=1, device_id=target, device_id_type=MESH_ID)
    convert_piece(0, lin, pieces.at[0])
    pl.semaphore_wait(barrier, 9)
    other = t + 1 - 2 * c

    def z_copy(w, d, s):
        step = 1 if d == 0 else -1
        src_t = t - 2 * step * s
        src = pieces.at[w, g] if s == 0 else weight_block(w, fulls[w], src_t, g)
        ok = (z - s >= 0) & (z + 1 < NZ) if d == 0 else (z + s < NZ) & (z - 1 >= 0)
        return ok, remote(src, weight_block(w, fulls[w], src_t, g), zs.at[w, d, s], zr.at[w, d, s], (g, t + 2 * step))

    def from_t(d, s):
        return t - 2 * (s + 1) if d == 0 else t + 2 * (s + 1)

    def here(d, s):
        return z - s - 1 >= 0 if d == 0 else z + s + 1 < NZ

    def z_wait(w, d, s):
        blk = weight_block(w, fulls[w], from_t(d, s), g)
        remote(blk, blk, zs.at[w, d, s], zr.at[w, d, s], (g, other)).wait_recv()

    def side_copy(w, d, s, axis):
        blk = weight_block(w, fulls[w], from_t(d, s), g)
        sems = (xs, xr) if axis == 0 else (ys, yr)
        return remote(blk, blk, sems[0].at[w, d, s], sems[1].at[w, d, s], (gx if axis == 0 else gy, t))

    def side_wait(w, d, s, axis):
        blk = weight_block(w, fulls[w], from_t(d, s), gx if axis == 0 else gy)
        sems = (xs, xr) if axis == 0 else (ys, yr)
        remote(blk, blk, sems[0].at[w, d, s], sems[1].at[w, d, s], (gx, t)).wait_recv()

    def diag_copy(w, d, s, axis):
        blk = weight_block(w, fulls[w], from_t(d, s), gx if axis == 0 else gy, axis)
        return remote(blk, blk, ds.at[w, d, s, axis], dr.at[w, d, s, axis], (gy if axis == 0 else gx, t))

    def diag_wait(w, d, s, axis):
        blk = weight_block(w, fulls[w], from_t(d, s), 3 - g, axis)
        remote(blk, blk, ds.at[w, d, s, axis], dr.at[w, d, s, axis], (gx, t)).wait_recv()

    def core_copy(w, d, s):
        blk = weight_strip(w, fulls[w], from_t(d, s))
        return remote(blk, blk, cs.at[w, d, s], cr.at[w, d, s], (g, other))

    def core_wait(w, d, s):
        blk = weight_strip(w, fulls[w], from_t(d, s) + 1 - 2 * c)
        remote(blk, blk, cs.at[w, d, s], cr.at[w, d, s], (g, other)).wait_recv()

    def own_copy(w):
        return remote(pieces.at[w], weight_strip(w, fulls[w], t), cs.at[w, 2, 0], cr.at[w, 2, 0], (g, other))

    def own_wait(w):
        blk = weight_strip(w, fulls[w], other)
        remote(blk, blk, cs.at[w, 2, 0], cr.at[w, 2, 0], (g, other)).wait_recv()

    def own_local(w):
        return pltpu.make_async_copy(pieces.at[w], weight_strip(w, fulls[w], t), ls.at[w])

    def both(s, fn):
        for d in (0, 1):
            @pl.when(here(d, s))
            def _():
                fn(d)

    def start_z(w, s):
        for d in (0, 1):
            ok, copy = z_copy(w, d, s)

            @pl.when(ok)
            def _():
                copy.start()

    def arrive(n):
        w, s = divmod(n, 3)
        both(s, lambda d: z_wait(w, d, s))
        if s < 2:
            start_z(w, s + 1)

        def sides(d):
            side_copy(w, d, s, 0).start()
            side_copy(w, d, s, 1).start()
        both(s, sides)
        if s == 0 and w < 2:
            start_z(w + 1, 0)
            own_copy(w + 1).start()

    def cross(n):
        w, s = divmod(n, 3)

        def fn(d):
            for axis in (0, 1):
                side_wait(w, d, s, axis)
                diag_copy(w, d, s, axis).start()
        both(s, fn)

    def finish(n):
        w, s = divmod(n, 3)

        def fn(d):
            diag_wait(w, d, s, 0)
            diag_wait(w, d, s, 1)
            core_copy(w, d, s).start()
        both(s, fn)

    def drain(w):
        own_wait(w)
        own_local(w).wait()
        for s in range(3):
            both(s, lambda d: core_wait(w, d, s))

    start_z(0, 0)
    own_copy(0).start()
    own_local(0).start()
    local_v = pltpu.make_async_copy(pv, wv.at[t], ls.at[3])
    local_v.start()
    v_copies = [remote(pv, wv.at[t], vs.at[k], vr.at[k], (g, peers[k])) for k in range(7)]
    for copy in v_copies:
        copy.start()
    for w in (1, 2):
        convert_piece(w, lin, pieces.at[w])
        own_local(w).start()
    fill_bias(bias)
    find_places(lens, line, column)
    att_in[...] = jnp.zeros_like(att_in)
    lse[...] = jnp.zeros_like(lse)
    arrive(0)
    local_v.wait()
    for k in range(7):
        remote(pv, wv.at[lax.rem(t + 7 - k, 8)], vs.at[k], vr.at[k], (g, peers[k])).wait_recv()
    for k in range(8):
        vec[:, ROWS * k : ROWS * k + ROWS] = wv[k, :, :ROWS]
        for j in range(4):
            lead = 4 * ROWS * k + ROWS * j
            fb1[0:1, lead : lead + ROWS] = wv[k, 8 + j : 9 + j, :ROWS]
    arrive(1)
    cross(0)
    norm_rows(tok, vec, att)
    move_rows(lambda first, count: to_places(line, first, count), att, normed)
    arrive(2)
    cross(1)
    finish(0)
    arrive(3)
    cross(2)
    finish(1)
    finish(2)
    drain(0)
    load = pltpu.make_async_copy(wa.at[pl.ds(0, 3)], wa_in, ls.at[4])
    load.start()
    load.wait()
    project_in(vec, wa_in, normed, proj)
    arrive(4)
    cross(3)
    events = [
        [(arrive, 5), (arrive, 6), (cross, 4), (finish, 3)],
        [(arrive, 7), (cross, 5), (finish, 4)],
        [(arrive, 8), (cross, 6), (finish, 5)],
        [(cross, 7), (finish, 6)],
        [(cross, 8), (finish, 7)],
        [(finish, 8)],
    ]
    for p in range(6):
        attend(p, proj, bias, att_in, lse)
        for event, n in events[p]:
            event(n)
    move_rows(lambda first, count: from_places(column, first, count), att_in, att)
    lse_out[...] = lse[...].T[:16]
    drain(1)
    drain(2)
    for copy in v_copies:
        copy.wait_send()
    for w in range(3):
        own_copy(w).wait_send()
        for s in range(3):
            for d in (0, 1):
                ok, copy = z_copy(w, d, s)

                @pl.when(ok)
                def _():
                    copy.wait_send()

            def sent(d):
                side_copy(w, d, s, 0).wait_send()
                side_copy(w, d, s, 1).wait_send()
                diag_copy(w, d, s, 0).wait_send()
                diag_copy(w, d, s, 1).wait_send()
                core_copy(w, d, s).wait_send()
            both(s, sent)


def front(lens, lin, pv, tok):
    vm = pl.BlockSpec(memory_space=pltpu.VMEM)
    rows = tok.shape[0]
    S = jax.ShapeDtypeStruct
    return pl.pallas_call(
        front_kernel,
        name="front",
        out_shape=[
            S((4, D, D), BF16), S((4, D, D), BF16), S((8, 4, ROWS, D), BF16),
            S((16, D), F32), S((8, MLP), F32),
            S((rows, D), BF16), S((3, rows, D), BF16), S((rows, D), BF16), S((16, rows), F32),
        ],
        in_specs=[pl.BlockSpec(memory_space=pltpu.SMEM)] + [vm] * 3,
        out_specs=[ANY] * 3 + [vm] * 6,
        scratch_shapes=[
            pltpu.VMEM((3, 4, ROWS, D), BF16),
            pltpu.VMEM((8, 16, 128), F32),
            pltpu.VMEM((3, D, D), BF16),
            pltpu.VMEM((4, 288, 384), F32),
            pltpu.VMEM((8, rows), jnp.int32),
            pltpu.VMEM((rows, 128), jnp.int32),
            pltpu.VMEM((rows, D), BF16),
            pltpu.VMEM((rows, 128), F32),
            DMA((5,)),
            DMA((3, 2, 3)), DMA((3, 2, 3)),
            DMA((3, 2, 3)), DMA((3, 2, 3)),
            DMA((3, 2, 3)), DMA((3, 2, 3)),
            DMA((3, 2, 3, 2)), DMA((3, 2, 3, 2)),
            DMA((3, 3, 3)), DMA((3, 3, 3)),
            DMA((7,)), DMA((7,)),
        ],
        compiler_params=pltpu.CompilerParams(collective_id=0, has_side_effects=True, vmem_limit_bytes=60 * 2**20),
    )(lens, lin, pv, tok)


def valid_rows(lens, first, count):
    total = jnp.int32(0)
    for j in range(lens.shape[1]):
        total = total + lens[0, j]
    at = lax.broadcasted_iota(jnp.int32, (count, 1), 0) + first
    return (at < total).astype(F32)


def forward_kernel(
    lens, tok_in, cot_in, att_in, wa, wb_in, wc_in, vec, fb1,
    bo_out, slope_out, n2_out, gc_out, vg,
    tok, cot, att, wp, wb, wc, bo, slope, n2, hid, gb2, gc, ls, os,
):
    pairs = [(att_in, att), (wa.at[3], wp), (tok_in, tok), (wb_in, wb), (wc_in, wc), (cot_in, cot)]
    loads = [pltpu.make_async_copy(src, dst, ls.at[i]) for i, (src, dst) in enumerate(pairs)]
    for copy in loads:
        copy.start()
    vg[...] = jnp.zeros_like(vg)
    rows = tok.shape[0]

    def row(j):
        return vec[j : j + 1, :]

    def stores(i):
        at = pl.ds(i * TILE, TILE)
        trio = [(bo, bo_out), (slope, slope_out), (n2, n2_out)]
        return [pltpu.make_async_copy(a.at[at, :], b.at[at, :], os.at[i, n]) for n, (a, b) in enumerate(trio)]

    for copy in loads[:3]:
        copy.wait()
    for i in range(rows // TILE):
        at = pl.ds(i * TILE, TILE)
        middle = tok[at, :] + row(5) * (nn(att[at, :], wp[...]) + row(4))
        normal, _inverse = normalize(middle)
        bo[at, :] = middle
        n2[at, :] = (normal * row(6) + row(7)).astype(BF16)
        if i == 0:
            loads[3].wait()

        def hidden(q, _):
            low = pl.ds(pl.multiple_of(q * D, D), D)
            pre = nn(n2[at, :], wb[q]) + fb1[0:1, low]
            h, s = gelu_and_slope(pre)
            hid[at, low] = h.astype(BF16)
            slope[at, low] = s.astype(BF16)
            return 0
        lax.fori_loop(0, 4, hidden, 0)
        if i == 0:
            loads[4].wait()
            loads[5].wait()
        branch_two = nn(hid[at, :], wc[...]) + row(12)
        bo[at, :] += row(13) * branch_two
        back = cot[at, :] * valid_rows(lens, i * TILE, TILE)
        low_back = (row(13) * back).astype(BF16)
        gb2[at, :] = low_back
        vg[13:14, :] += col_sum(back * branch_two)
        vg[12:13, :] += col_sum(low_back.astype(F32))
        for copy in stores(i):
            copy.start()

    def fc2(t, _):
        low = pl.ds(pl.multiple_of(t * 384, 128), 384)
        gc[t] = tn(hid[:, low], gb2[...]).astype(BF16).reshape(4, ROWS, D)
        return 0
    lax.fori_loop(0, 8, fc2, 0)
    store = pltpu.make_async_copy(gc, gc_out, os.at[4, 0])
    store.start()
    for i in range(rows // TILE):
        for copy in stores(i):
            copy.wait()
    store.wait()


def forward(lens, tok, cot, att, wa, wb, wc, vec, fb1):
    vm = pl.BlockSpec(memory_space=pltpu.VMEM)
    rows = tok.shape[0]
    S = jax.ShapeDtypeStruct
    V = pltpu.VMEM
    return pl.pallas_call(
        forward_kernel,
        name="mlp_forward",
        out_shape=[S((rows, D), F32), S((rows, MLP), BF16), S((rows, D), BF16), S((8, 4, ROWS, D), BF16), S((16, D), F32)],
        in_specs=[pl.BlockSpec(memory_space=pltpu.SMEM)] + [ANY] * 6 + [vm] * 2,
        out_specs=[ANY] * 4 + [vm],
        scratch_shapes=[
            V((rows, D), F32), V((rows, D), F32), V((rows, D), BF16), V((D, D), BF16),
            V((4, D, D), BF16), V((MLP, D), BF16), V((rows, D), F32), V((rows, MLP), BF16),
            V((rows, D), BF16), V((rows, MLP), BF16), V((rows, D), BF16), V((8, 4, ROWS, D), BF16),
            DMA((6,)), DMA((5, 3)),
        ],
        compiler_params=pltpu.CompilerParams(vmem_limit_bytes=62 * 2**20),
    )(lens, tok, cot, att, wa, wb, wc, vec, fb1)


ORDER = (2, 1, 0)


def back_kernel(
    lens, vec, vg_in, tok, cot, wa, wb_in, wc_in, att_in, slope_in, n2_in, normed_in, proj_in, lse_in, gc,
    gin, lin_out, sv, sq,
    line, column, wide, tall, gatt, gout, gb, own, core, zbuf, vg, vg1, gv, vbuf, qbuf,
    ls, os, cs, cr, zs, zr, vs, vr, qs, qr,
):
    g, t, z, c, gx, gy = place()
    peers = [lax.rem(t + k, 8) for k in range(1, 8)]
    rows = tok.shape[0]
    other = t + 1 - 2 * c

    def local(pairs, first):
        return [pltpu.make_async_copy(src, dst, ls.at[first + i]) for i, (src, dst) in enumerate(pairs)]

    loads = local([(tok, wide), (cot, tall)], 0)
    for copy in loads:
        copy.start()
    greet([(g, p) for p in peers], 7)

    def own_at(w, k):
        return (gout.at[2 * k + c], gb.at[2 * k + c], own.at[k])[w]

    def core_copy(w, k):
        return remote((gout, gb, gc)[w].at[2 * k + 1 - c], core.at[w, k], cs.at[w, k], cr.at[w, k], (g, other))

    def load(k):
        return pltpu.make_async_copy(gc.at[2 * k + c], own.at[k], os.at[k])

    def begin(w):
        for k in (3, 0, 2, 1):
            core_copy(w, k).start()
            if w == 2:
                load(k).start()

    def slot(d, k, to):
        return k - to if d == 0 else 4 - (to - k)

    def total_of(w, k, q, at, extra):
        mine = own_at(w, k)
        total = mine[q, at, :].astype(F32) + core[w, k, q, at, :].astype(F32)
        for d in extra:
            total = total + zbuf[w, slot(d, k, z), q, at, :].astype(F32)
        return total

    def add_rows(w, k, h, extra):
        for q in (2 * h, 2 * h + 1):
            def body(i, _):
                at = pl.ds(pl.multiple_of(i * 32, 32), 32)
                own_at(w, k)[q, at, :] = total_of(w, k, q, at, extra).astype(BF16)
                return 0
            lax.fori_loop(0, ROWS // 32, body, 0)

    def lay_out(lin, w, k, h, extra):
        for q in (2 * h, 2 * h + 1):
            if w == 2:
                base, stride = 4608 + 576 * q, 6
            elif w == 1:
                base, stride = 2304 + 6 * q, 24
            else:
                base, stride = (1728, 6) if q == 3 else (6 * q, 18)

            def body(i, _):
                at = pl.ds(pl.multiple_of(i * 32, 32), 32)
                total = total_of(w, k, q, at, extra)
                for m in range(6):
                    lin[pl.ds(base + m + i * (32 * stride), 32, stride=stride), :] = total[:, 128 * m : 128 * m + 128]
                return 0
            lax.fori_loop(0, ROWS // 32, body, 0)

    def z_copy(w, d, k, h):
        step = 1 if d == 0 else -1
        at = pl.ds(2 * h, 2)
        return remote(
            own_at(w, k).at[at],
            zbuf.at[w, slot(d, k, z + step), at],
            zs.at[w, d, k, h],
            zr.at[w, d, k, h],
            (g, t + 2 * step),
        )

    def z_wait(w, d, k, h):
        here = zbuf.at[w, slot(d, k, z), pl.ds(2 * h, 2)]
        remote(here, here, zs.at[w, d, k, h], zr.at[w, d, k, h], (g, other)).wait_recv()

    def ready(w, k):
        if w == 2:
            load(k).wait()
        core_copy(w, k).wait_recv()

    def pass_on(i, d, j, h):
        w = ORDER[i]
        reach = NZ - 1 - z if d == 0 else z
        k = z + j if d == 0 else z - j
        first = z == 0 if d == 0 else z == NZ - 1

        @pl.when(j <= reach)
        def _():
            if h == 0:
                ready(w, k)

            @pl.when(first)
            def _():
                add_rows(w, k, h, ())

            @pl.when(jnp.logical_not(first))
            def _():
                z_wait(w, d, k, h)
                add_rows(w, k, h, (d,))

            if i > 0:
                @pl.when(j == reach)
                def _():
                    z_copy(ORDER[i - 1], d, z + 1 if d == 0 else z - 1, h).wait_send()
            if j < NZ - 1:
                @pl.when(j < reach)
                def _():
                    z_copy(w, d, k + 1 if d == 0 else k - 1, h).wait_send()
            z_copy(w, d, k, h).start()

    def settle(lin, i):
        w = ORDER[i]
        ready(w, z)
        for h in (0, 1):
            for cond, dirs in ((z == 0, (1,)), (z == NZ - 1, (0,)), ((z > 0) & (z < NZ - 1), (0, 1))):
                @pl.when(cond)
                def _():
                    for d in dirs:
                        z_wait(w, d, z, h)
                    lay_out(lin, w, z, h, dirs)

    steps = [(i, j, h) for i in range(3) for j in (3, 2, 1) for h in (0, 1)]

    def run(lo, hi):
        for i, j, h in steps[lo:hi]:
            pass_on(i, 0, j, h)
            pass_on(i, 1, j, h)

    begin(2)
    find_places(lens, line, column)
    vg[...] = vg_in[...]
    vg1[...] = jnp.zeros_like(vg1)

    def mlp_part(wp, wb, wc, grads, n2, att, gb1):
        inner = local(
            [(att_in, att), (wa.at[3], wp), (wc_in, wc), (slope_in, grads), (wb_in, wb), (n2_in, n2)], 2
        )
        for copy in inner:
            copy.start()
        run(0, 2)
        for copy in loads + inner:
            copy.wait()

        def row(j):
            return vec[j : j + 1, :]

        def tile(i):
            at = pl.ds(i * TILE, TILE)
            branch_one = nn(att[at, :], wp[...]) + row(4)
            normal, inverse = normalize(wide[at, :] + row(5) * branch_one)
            tall[at, :] = tall[at, :] * valid_rows(lens, i * TILE, TILE)
            low_back = (row(13) * tall[at, :]).astype(BF16)

            def backward(q, total):
                low = pl.ds(pl.multiple_of(q * D, D), D)
                grad = nt(low_back, wc[low, :]) * grads[at, low].astype(F32)
                grad = grad.astype(BF16)
                grads[at, low] = grad
                vg1[0:1, low] += col_sum(grad.astype(F32))
                return total + nt(grad, wb[q])
            grad_n2 = lax.fori_loop(0, 4, backward, jnp.zeros((TILE, D), F32))
            vg[6:7, :] += col_sum(grad_n2 * normal)
            vg[7:8, :] += col_sum(grad_n2)
            grad_mid = tall[at, :] + norm_pull(grad_n2, normal, inverse, row(6))
            tall[at, :] = grad_mid
            vg[5:6, :] += col_sum(grad_mid * branch_one)
            low_one = (row(5) * grad_mid).astype(BF16)
            gb1[at, :] = low_one
            vg[4:5, :] += col_sum(low_one.astype(F32))
            gatt[at, :] = nt(low_one, wp[...]).astype(BF16)

        for i in range(rows // TILE):
            tile(i)
            run(2 + i, 3 + i)

        def fc1(q, _):
            def part(m, _):
                low = pl.ds(pl.multiple_of(q * D + m * 384, 128), 384)
                col = pl.ds(pl.multiple_of(m * 384, 128), 384)
                gb[:, q, :, col] = tn(n2[...], grads[:, low]).astype(BF16).reshape(8, ROWS, 384)
                return 0
            return lax.fori_loop(0, 2, part, 0)
        lax.fori_loop(0, 4, fc1, 0)
        begin(1)

        def proj_part(m, _):
            col = pl.ds(pl.multiple_of(m * 384, 128), 384)
            gout[:, 3, :, col] = tn(att[...], gb1[:, col]).astype(BF16).reshape(8, ROWS, 384)
            return 0
        lax.fori_loop(0, 2, proj_part, 0)

    pl.run_scoped(
        mlp_part,
        pltpu.VMEM((D, D), BF16),
        pltpu.VMEM((4, D, D), BF16),
        pltpu.VMEM((MLP, D), BF16),
        pltpu.VMEM((rows, MLP), BF16),
        pltpu.VMEM((rows, D), BF16),
        pltpu.VMEM((rows, D), BF16),
        pltpu.VMEM((rows, D), BF16),
    )
    v_copies = [remote(gv.at[peers[k]], vbuf.at[k], vs.at[k], vr.at[k], (g, peers[k])) for k in range(7)]
    q_copies = [remote(qbuf.at[7], qbuf.at[k], qs.at[k], qr.at[k], (g, peers[k])) for k in range(7)]

    def attention_part(lin, bias, lse_t, gatt_at, dq, wa_v, normed, proj):
        inner = local([(proj_in, proj), (lse_in, lse_t), (wa.at[pl.ds(0, 3)], wa_v), (normed_in, normed)], 8)
        for copy in inner:
            copy.start()
        run(6, 7)
        fill_bias(bias)
        move_rows(lambda first, count: to_places(line, first, count), gatt, gatt_at)
        for copy in inner:
            copy.wait()
        for p in range(6):
            attend_back(p, proj, gatt_at, bias, lse_t, dq)
            if p == 0:
                settle(lin, 0)
            if p < 5:
                run(7 + p, 8 + p)
        weight_grads(normed, proj, gout)
        begin(0)
        row_grads(column, wide, tall, vec, wa_v, proj, vg)
        store = pltpu.make_async_copy(tall, gin, ls.at[12])
        store.start()
        for k in range(8):
            gv[k, :, :ROWS] = vg[:, ROWS * k : ROWS * k + ROWS]
            for j in range(4):
                lead = 4 * ROWS * k + ROWS * j
                gv[k, 8 + j : 9 + j, :ROWS] = vg1[0:1, lead : lead + ROWS]
        run(12, 13)
        for copy in v_copies:
            copy.start()
        settle(lin, 1)
        run(13, 18)
        for k in range(7):
            v_copies[k].wait_recv()
        total = gv[t]
        for k in range(7):
            total = total + vbuf[k]
        lane = lax.broadcasted_iota(jnp.int32, (16, 128), 1)
        across = lax.broadcasted_iota(jnp.int32, (16, 128), 0)
        total = jnp.where((lane < ROWS) & (across < 14), total, 0.0)
        sv[...] = total
        settle(lin, 2)
        lin_store = pltpu.make_async_copy(lin, lin_out, ls.at[13])
        lin_store.start()

        def square(i, acc):
            v = lin[pl.ds(pl.multiple_of(i * 64, 64), 64), :]
            return acc + v * v
        acc = lax.fori_loop(0, 108, square, jnp.zeros((64, 128), F32))
        qbuf[7] = jnp.full((8, 128), jnp.sum(acc) + jnp.sum(total * total), F32)
        for copy in q_copies:
            copy.start()
        store.wait()
        lin_store.wait()

    pl.run_scoped(
        attention_part,
        pltpu.VMEM((6912, 128), F32),
        pltpu.VMEM((4, 288, 384), F32),
        pltpu.VMEM((16, rows), F32),
        pltpu.VMEM((rows, D), BF16),
        pltpu.VMEM((rows, 128), F32),
        pltpu.VMEM((3, D, D), BF16),
        pltpu.VMEM((rows, D), BF16),
        pltpu.VMEM((3, rows, D), BF16),
    )
    for w in range(3):
        for k in range(NZ):
            core_copy(w, k).wait_send()
    for h in (0, 1):
        @pl.when(z < NZ - 1)
        def _():
            z_copy(0, 0, z + 1, h).wait_send()

        @pl.when(z > 0)
        def _():
            z_copy(0, 1, z - 1, h).wait_send()
    for k in range(7):
        q_copies[k].wait_recv()
    acc = qbuf[7]
    for k in range(7):
        acc = acc + qbuf[k]
    sq[...] = acc
    for k in range(7):
        q_copies[k].wait_send()
        v_copies[k].wait_send()


def back(lens, vec, vg, tok, cot, wa, wb, wc, att, slope, n2, normed, proj, lse_t, gc):
    vm = pl.BlockSpec(memory_space=pltpu.VMEM)
    rows = tok.shape[0]
    S = jax.ShapeDtypeStruct
    V = pltpu.VMEM
    return pl.pallas_call(
        back_kernel,
        name="back",
        out_shape=[S((rows, D), F32), S((6912, 128), F32), S((16, 128), F32), S((8, 128), F32)],
        in_specs=[pl.BlockSpec(memory_space=pltpu.SMEM)] + [vm] * 2 + [ANY] * 12,
        out_specs=[ANY] * 2 + [vm] * 2,
        scratch_shapes=[
            V((8, rows), jnp.int32),
            V((rows, 128), jnp.int32),
            V((rows, D), F32),
            V((rows, D), F32),
            V((rows, D), BF16),
            V((8, 4, ROWS, D), BF16),
            V((8, 4, ROWS, D), BF16),
            V((NZ, 4, ROWS, D), BF16),
            V((3, NZ, 4, ROWS, D), BF16),
            V((3, 5, 4, ROWS, D), BF16),
            V((16, D), F32),
            V((8, MLP), F32),
            V((8, 16, 128), F32),
            V((7, 16, 128), F32),
            V((8, 8, 128), F32),
            DMA((14,)), DMA((NZ,)), DMA((3, NZ)), DMA((3, NZ)),
            DMA((3, 2, NZ, 2)), DMA((3, 2, NZ, 2)),
            DMA((7,)), DMA((7,)), DMA((7,)), DMA((7,)),
        ],
        compiler_params=pltpu.CompilerParams(
            collective_id=1, has_side_effects=True, vmem_limit_bytes=63 * 2**20
        ),
    )(lens, vec, vg, tok, cot, wa, wb, wc, att, slope, n2, normed, proj, lse_t, gc)


PARTS = 6912
SUM_H, SUM_Q, SUM_E = PARTS // 2, PARTS // 4, PARTS // 8
MATRIX_WIDTH = PARTS * 128
VECTOR_WIDTH = 14 * ROWS


def finish_kernel(
    grad, sv, sq, master, first, second, outer,
    first_new, second_new, mean_out, outer_new, weights_new, vector_out, norm_out,
    b_master, b_first, b_second, b_outer, b_mean, diff, mean, part, mid, buf, tail_grad, tail, ls, os, ss, rs, ts, tr,
):
    g, t, z, c, gx, gy = place()
    pairs = [(master, b_master.at[0]), (first, b_first), (second, b_second), (outer, b_outer.at[0])]
    loads = [pltpu.make_async_copy(src, dst, ls.at[i]) for i, (src, dst) in enumerate(pairs)]
    for copy in loads:
        copy.start()
    peers = [gx, gy, 3 - g]
    barrier = pltpu.get_barrier_semaphore()
    for peer in peers:
        pl.semaphore_signal(barrier, inc=1, device_id=(peer, t), device_id_type=MESH_ID)
    norm = jnp.sqrt(sq[0:1, 0:1])
    norm_out[...] = jnp.broadcast_to(norm, (8, 128))
    scale = clip_limit / (norm + 1e-06)
    for j in range(14):
        tail_grad[0:1, ROWS * j : ROWS * j + ROWS] = sv[j : j + 1, :ROWS]
    vector_out[...] = tail_grad[...] / jnp.sqrt(F32(8 * 1024))
    xi, yi = lax.rem(g, 2), lax.div(g, 2)
    hop = [((gx, t), (gy, t)), ((gy, t), (gx, t))]
    mine = [(xi, yi), (yi, xi)]

    def line(at):
        return pl.ds(pl.multiple_of(at.start * 128, 1024), at.size * 128)

    step_rate = base_rate * rate_scale

    def adam(value, old_first, old_second, weight, decay):
        clipped = value * scale
        new_first = beta_first * old_first + (1.0 - beta_first) * clipped
        new_second = beta_second * old_second + (1.0 - beta_second) * clipped * clipped
        root = jnp.sqrt(new_second * (1.0 / (1.0 - beta_second**adam_count))) + adam_epsilon
        ahead = new_first * (1.0 / (1.0 - beta_first**adam_count)) / root
        if decay:
            ahead = ahead + weight_decay * weight
        return new_first, new_second, step_rate * ahead

    def nesterov(weight, momentum, average):
        new_momentum = outer_beta * momentum + average
        return new_momentum, weight - outer_rate * (average + outer_beta * new_momentum)

    def rows_loop(lo, count, fn):
        chunk = 48

        def body(i, _):
            fn(pl.ds(pl.multiple_of(lo + i * chunk, 16), chunk), pl.ds(pl.multiple_of(i * chunk, 16), chunk))
            return 0
        lax.fori_loop(0, count // chunk, body, 0)

    def adam_rows(lo, count):
        def fn(at, _):
            flat = line(at)
            b_first[:, flat], b_second[:, flat], ahead = adam(
                grad[at, :].reshape(1, -1), b_first[:, flat], b_second[:, flat], b_master[:, flat], True
            )
            diff[at, :] = ahead.reshape(-1, 128).astype(BF16)
        rows_loop(lo, count, fn)

    def outer_rows(lo, count):
        def fn(at, _):
            flat = line(at)
            average = mean[at, :].astype(F32).reshape(1, -1)
            b_mean[:, flat] = average
            b_outer[:, flat], b_master[:, flat] = nesterov(b_master[:, flat], b_outer[:, flat], average)
        rows_loop(lo, count, fn)

    def copies(h):
        a, b = mine[h]
        base = h * SUM_H
        sent = rows_at(diff, base + (1 - a) * SUM_Q, SUM_Q)
        one = remote(sent, part.at[h], ss.at[h, 0], rs.at[h, 0], hop[h][0])
        two = remote(rows_at(mid.at[h], (1 - b) * SUM_E, SUM_E), buf.at[h], ss.at[h, 1], rs.at[h, 1], hop[h][1])
        done = rows_at(mean, base + a * SUM_Q + b * SUM_E, SUM_E)
        three = remote(done, done, ss.at[h, 2], rs.at[h, 2], hop[h][1])
        whole = rows_at(mean, base + a * SUM_Q, SUM_Q)
        four = remote(whole, whole, ss.at[h, 3], rs.at[h, 3], hop[h][0])
        return one, two, three, four

    steps = [copies(0), copies(1)]
    for copy in loads[:3]:
        copy.wait()
    for h in (0, 1):
        adam_rows(h * SUM_H + (1 - mine[h][0]) * SUM_Q, SUM_Q)
        if h == 0:
            pl.semaphore_wait(barrier, 3)
        steps[h][0].start()
    at_tail = pl.ds(MATRIX_WIDTH, VECTOR_WIDTH)
    new_first, new_second, ahead = adam(tail_grad[...], b_first[:, at_tail], b_second[:, at_tail], None, False)
    b_first[:, at_tail] = new_first
    b_second[:, at_tail] = new_second
    tail[3, :, :] = jnp.zeros((1, 1408), F32)
    tail[3, :, pl.ds(0, VECTOR_WIDTH)] = ahead
    t_copies = [remote(tail.at[3], tail.at[k], ts.at[k], tr.at[k], (peers[k], t)) for k in range(3)]
    for copy in t_copies:
        copy.start()
    for h in (0, 1):
        adam_rows(h * SUM_H + mine[h][0] * SUM_Q, SUM_Q)
    stores = [pltpu.make_async_copy(b_first, first_new, os.at[0]), pltpu.make_async_copy(b_second, second_new, os.at[1])]
    for copy in stores:
        copy.start()
    for h in (0, 1):
        a, b = mine[h]
        steps[h][0].wait_recv()
        lo = (1 - b) * SUM_E
        src = h * SUM_H + a * SUM_Q + lo

        def fn(at, local):
            here = pl.ds(pl.multiple_of(lo + local.start, 16), local.size)
            mid[h, here, :] = (diff[at, :].astype(F32) + part[h, here, :].astype(F32)).astype(BF16)
        rows_loop(src, SUM_E, fn)
        steps[h][1].start()
    loads[3].wait()
    for h in (0, 1):
        a, b = mine[h]
        steps[h][1].wait_recv()
        lo = b * SUM_E
        src = h * SUM_H + a * SUM_Q + lo

        def fn(at, local):
            here = pl.ds(pl.multiple_of(lo + local.start, 16), local.size)
            total = diff[at, :].astype(F32) + part[h, here, :].astype(F32) + buf[h, local, :].astype(F32)
            mean[at, :] = (total * 0.25).astype(BF16)
        rows_loop(src, SUM_E, fn)
        steps[h][2].start()
    for copy in t_copies:
        copy.wait_recv()
    total = tail[3] + tail[0] + tail[1] + tail[2]
    average = total[:, :VECTOR_WIDTH] * 0.25
    b_mean[:, at_tail] = average
    new_momentum, new_weights = nesterov(b_master[:, at_tail], b_outer[:, at_tail], average)
    b_outer[:, at_tail] = new_momentum
    b_master[:, at_tail] = new_weights
    for h in (0, 1):
        a, b = mine[h]
        outer_rows(h * SUM_H + a * SUM_Q + b * SUM_E, SUM_E)
    for h in (0, 1):
        a, b = mine[h]
        rest = h * SUM_H + a * SUM_Q + (1 - b) * SUM_E
        other = rows_at(mean, rest, SUM_E)
        remote(other, other, ss.at[h, 2], rs.at[h, 2], hop[h][1]).wait_recv()
        steps[h][2].wait_send()
        steps[h][3].start()
        outer_rows(rest, SUM_E)
    for h in (0, 1):
        a, b = mine[h]
        rest = h * SUM_H + (1 - a) * SUM_Q
        other = rows_at(mean, rest, SUM_Q)
        remote(other, other, ss.at[h, 3], rs.at[h, 3], hop[h][0]).wait_recv()
        outer_rows(rest, SUM_Q)
    last = [
        pltpu.make_async_copy(b_mean.at[0], mean_out, os.at[2]),
        pltpu.make_async_copy(b_outer.at[0], outer_new, os.at[3]),
        pltpu.make_async_copy(b_master.at[0], weights_new, os.at[4]),
    ]
    for copy in last:
        copy.start()
    for h in (0, 1):
        steps[h][0].wait_send()
        steps[h][1].wait_send()
        steps[h][3].wait_send()
    for copy in t_copies:
        copy.wait_send()
    for copy in stores + last:
        copy.wait()


def finish(grad, sv, sq, master, first, second, outer):
    vm = pl.BlockSpec(memory_space=pltpu.VMEM)
    S = jax.ShapeDtypeStruct
    n = master.shape[0]
    flat = pltpu.VMEM((1, n), F32)
    return pl.pallas_call(
        finish_kernel,
        name="finish",
        out_shape=[S((1, n), F32)] * 2 + [S((n,), F32)] * 3 + [S((1, VECTOR_WIDTH), F32), S((8, 128), F32)],
        in_specs=[vm] * 3 + [ANY] * 4,
        out_specs=[ANY] * 5 + [vm] * 2,
        scratch_shapes=[flat] * 5
        + [
            pltpu.VMEM((PARTS, 128), BF16),
            pltpu.VMEM((PARTS, 128), BF16),
            pltpu.VMEM((2, SUM_Q, 128), BF16),
            pltpu.VMEM((2, SUM_Q, 128), BF16),
            pltpu.VMEM((2, SUM_E, 128), BF16),
            pltpu.VMEM((1, VECTOR_WIDTH), F32),
            pltpu.VMEM((4, 1, 1408), F32),
            DMA((4,)), DMA((5,)), DMA((2, 4)), DMA((2, 4)), DMA((3,)), DMA((3,)),
        ],
        compiler_params=pltpu.CompilerParams(collective_id=2, has_side_effects=True, vmem_limit_bytes=60 * 2**20),
    )(grad, sv, sq, master, first, second, outer)


def on_small_slice(tokens, cotangent, crop_lengths, master, first_moment, second_moment, outer_momentum):
    lin = master[:MATRIX_WIDTH].reshape(-1, 128)
    vector = master[MATRIX_WIDTH:].astype(BF16).astype(F32).reshape(14, ROWS)
    piece = jnp.pad(vector, ((0, 2), (0, 128 - ROWS)))
    wa, wb, wc, vec, fb1, normed, projected, attended, lse = front(crop_lengths, lin, piece, tokens)
    block_output, slope, normed_two, grad_fc2, vg = forward(
        crop_lengths, tokens, cotangent, attended, wa, wb, wc.reshape(MLP, D), vec, fb1
    )
    input_grad, grad_lin, sv, sq = back(
        crop_lengths, vec, vg, tokens, cotangent, wa, wb, wc.reshape(MLP, D), attended, slope, normed_two, normed,
        projected, lse, grad_fc2
    )
    moment_one, moment_two, mean_difference, outer_new, new_weights, vector_part, norm = finish(
        grad_lin, sv, sq, master, first_moment, second_moment, outer_momentum
    )
    return (
        block_output,
        input_grad,
        norm[0, :1],
        vector_part,
        moment_one,
        moment_two,
        mean_difference,
        outer_new,
        new_weights,
    )


def solution(mesh):
    small = mesh.shape["grp"] == 4 and mesh.shape["tok"] == 8
    return jax.shard_map(
        on_small_slice if small else on_device,
        mesh=mesh,
        in_specs=(
            P(("grp", "tok"), None),
            P(("grp", "tok"), None),
            P(("grp", "tok"), None),
            P("tok"),
            P("grp", "tok"),
            P("grp", "tok"),
            P("tok"),
        ),
        out_specs=(
            P(("grp", "tok"), None),
            P(("grp", "tok"), None),
            P("grp"),
            P("grp", "tok"),
            P("grp", "tok"),
            P("grp", "tok"),
            P("tok"),
            P("tok"),
            P("tok"),
        ),
        check_vma=False,
    )
```

profile of v0, /device:TPU:0, one launch (start us, length us, event | category | flops | bytes accessed | tf_op | source)
XLA Modules:
  0.0 332.1 jit_solution(17665894808083753060)
XLA Ops:
  0.6 4.0 %slice_bitcast_fusion.lin = f32[6912,128]{1,0:T(8,128)} fusion(f32[886080]{0:T(1024)} %master.1), kind=kLoop, calls=%fused_computation | loop fusion | bytes 7077888 | tf_op jit(solution)/shard_map/reshape | solution.py:1423
  4.7 0.7 slice.24
  5.4 0.1 convert_element_type.10
  5.5 0.6 pad_convert_fusion.pv
  6.1 80.5 %front.1 = (bf16[4,768,768]{2,1,0:T(8,128)(2,1)}, bf16[4,768,768]{2,1,0:T(8,128)(2,1)}, bf16[8,4,96,768]{3,2,1,0:T(8,128)(2,1)}, f32[16,768]{1,0:T(8,128)}, f32[...) custom-call(s32[1,10]{1,0:T(1,128)} %lens.5, ...), custom_call_target="tpu_custom_call" | custom-call | tf_op jit(solution)/shard_map/front/pallas_call | solution.py:758
  86.6 33.2 %mlp_forward.1 = (f32[1024,768]{1,0:T(8,128)}, bf16[1024,3072]{1,0:T(8,128)(2,1)}, bf16[1024,768]{1,0:T(8,128)(2,1)}, bf16[8,4,96,768]{3,2,1,0:T(8,128)(2,1)}, f32[16,768]{1,0:T(8,128)}) custom-call(s32[1,10]{1,0:T(1,128)} %lens.5, f32[1024,768]{1,0:T(8,128)} %tok.3, f32[1024,768]{1,0:T(8,128)} %cot.1, bf16[1024,768]{1,0:T(8,128)(2,1)} %get-tuple-element.34.att_in, ...), custom_call_target="tpu_custom_call" | custom-call | tf_op jit(solution)/shard_map/mlp_forward/pallas_call | solution.py:867
  119.7 140.6 %back.1 = (f32[1024,768]{1,0:T(8,128)}, f32[6912,128]{1,0:T(8,128)}, f32[16,128]{1,0:T(8,128)}, f32[8,128]{1,0:T(8,128)}) custom-call(s32[1,10]{1,0:T(1,128)} %lens.5, f32[16,768]{1,0:T(8,128)} %get-tuple-element.38.vec, f32[16,768]{1,0:T(8,128)} %get-tuple-element.41.vg_in, f32[1024,768]{1,0:T(8,128)} %tok.3, f32[1024,768]{1,0:T(8,128)} %cot.1, ...), custom_call_target="tpu_custom_call" | custom-call | tf_op jit(solution)/shard_map/back/pallas_call | solution.py:1190
  260.4 0.0 copy-start.5
  260.4 52.7 %finish.1 = (f32[1,886080]{1,0:T(1,128)}, f32[1,886080]{1,0:T(1,128)}, f32[886080]{0:T(1024)}, f32[886080]{0:T(1024)}, f32[886080]{0:T(1024)}, /*index=5*/f32[1,1344]{1,0:T(1,128)}, f32[8,128]{1,0:T(8,128)}) custom-call(f32[6912,128]{1,0:T(8,128)} %get-tuple-element.49.grad, f32[16,128]{1,0:T(8,128)} %get-tuple-element.50.sv, ...), custom_call_target="tpu_custom_call" | custom-call | tf_op jit(solution)/shard_map/finish/pallas_call | solution.py:1401
  313.1 0.0 copy-start.6
  313.1 0.0 copy-start.4
  313.1 1.3 slice.20
  314.4 0.0 copy-done.5
  314.4 1.7 copy.23
  316.1 0.0 copy-done.6
  316.1 0.6 copy.24
  316.7 0.0 copy-done.4
  316.7 0.0 copy-start.3
  316.7 1.8 copy.25
  318.5 1.5 copy-done.3
  320.0 0.0 copy-start.2
  320.0 1.8 copy.26
  321.8 1.5 copy-done.2
  323.3 0.0 copy-start.1
  323.3 2.0 copy.27
  325.3 1.2 copy-done.1
  326.5 0.0 copy-start
  326.5 2.0 copy.28
  328.6 1.2 copy-done
  329.8 2.0 copy.29
Async XLA Ops:
  260.4 54.0 %copy-start.5 = (f32[1024,768]{1,0:T(8,128)S(1)}, f32[1024,768]{1,0:T(8,128)}, u32[]{:S(2)}) copy-start(f32[1024,768]{1,0:T(8,128)} %get-tuple-element.69) | copy-start | bytes 9437188
  313.1 3.0 copy-start.6
  313.1 3.6 %copy-start.4 = (f32[1,886080]{1,0:T(1,128)S(1)}, f32[1,886080]{1,0:T(1,128)}, u32[]{:S(2)}) copy-start(f32[1,886080]{1,0:T(1,128)} %get-tuple-element.72) | copy-start | bytes 10632964
  316.7 3.3 copy-start.3
  320.0 3.3 copy-start.2
  323.3 3.3 copy-start.1
  326.5 3.3 copy-start
where the time goes:
time: 336 us; the launch traced here: 332 us
  Pallas kernels  307 us (91%)
  local copies, waits for them, and re-layouts  23.6 us (7%)
    pallas_call x1, Pallas kernels, back(): pl.pallas_call(back_kernel, name='back', out_shape=[S((rows, D), F32), S(...  141 us
    pallas_call x1, Pallas kernels, front(): pl.pallas_call(front_kernel, name='front', out_shape=[S((4, D, D), BF16),...  80.5 us
    pallas_call x1, Pallas kernels, finish(): pl.pallas_call(finish_kernel, name='finish', out_shape=[S((1, n), F32)] *...  52.7 us
    pallas_call x1, Pallas kernels, forward(): pl.pallas_call(forward_kernel, name='mlp_forward', out_shape=[S((rows, D)...  33.2 us
    unnamed x21, local copies, waits for them, and re-layouts  17.4 us

commit v1 on v0

--- a/solution.py
+++ b/solution.py
@@ -304,6 +304,7 @@
 def rows_at(ref, start, count):
     return ref.at[pl.ds(pl.multiple_of(start, 16), count), :]
 
+
 TILE = 256
 
 
@@ -538,32 +539,48 @@
             piece[q, :, 128 * m : 128 * m + 128] = lin[at, :].astype(BF16)
 
 
+def to_rows(flat, lin, first, count):
+    def body(i, _):
+        at = first + i * 48
+        value = flat[:, pl.ds(pl.multiple_of(at * 128, 6144), 6144)]
+        lin[pl.ds(pl.multiple_of(at, 48), 48), :] = value.reshape(48, 128)
+        return 0
+    lax.fori_loop(0, count // 48, body, 0)
+
+
 def weight_strip(w, ref, t):
     if w == 2:
         return ref.at[t]
     return ref.at[:, pl.ds(pl.multiple_of(t * ROWS, 16), ROWS), :]
 
 
-def weight_block(w, ref, t, q, half=None):
-    lead, count = (0, ROWS) if half is None else (48 * half, 48)
+def weight_block(w, ref, t, q, lead=0, count=ROWS):
     if w == 2:
         return ref.at[t, q, pl.ds(lead, count), :]
     return ref.at[q, pl.ds(pl.multiple_of(t * ROWS + lead, 16), count), :]
 
 
 def front_kernel(
-    lens, lin, pv, tok,
+    lens, master, tok,
     wa, wb, wc, vec, fb1, normed, proj, att, lse_out,
-    pieces, wv, wa_in, bias, line, column, att_in, lse,
-    ls, zs, zr, xs, xr, ys, yr, ds, dr, cs, cr, vs, vr,
+    flat, lin, pv, pieces, wv, wa_in, bias, line, column, att_in, lse,
+    ls, zs, zr, xs, xr, ys, yr, ds, dr, cs, cr, vs, vr, es, er,
 ):
+    weights_in = pltpu.make_async_copy(master, flat.at[0], ls.at[5])
+    weights_in.start()
     g, t, z, c, gx, gy = place()
     fulls = (wa, wb, wc)
     peers = [lax.rem(t + k, 8) for k in range(1, 8)]
     barrier = pltpu.get_barrier_semaphore()
     for target in [(g, p) for p in peers] + [(gx, t), (gy, t)]:
         pl.semaphore_signal(barrier, inc=1, device_id=target, device_id_type=MESH_ID)
+    weights_in.wait()
+    to_rows(flat, lin, 0, 2304)
     convert_piece(0, lin, pieces.at[0])
+    pv[...] = jnp.zeros_like(pv)
+    for j in range(14):
+        low = flat[:, pl.ds(6912 * 128 + ROWS * j, ROWS)].astype(BF16)
+        pv[j : j + 1, :ROWS] = low.astype(F32)
     pl.semaphore_wait(barrier, 9)
     other = t + 1 - 2 * c
 
@@ -574,6 +591,18 @@
         ok = (z - s >= 0) & (z + 1 < NZ) if d == 0 else (z + s < NZ) & (z - 1 >= 0)
         return ok, remote(src, weight_block(w, fulls[w], src_t, g), zs.at[w, d, s], zr.at[w, d, s], (g, t + 2 * step))
 
+    def extra_copy(w, d, s):
+        step = 1 if d == 0 else -1
+        src_t = t - 2 * step * s
+        src = pieces.at[w, 3 - g, pl.ds(0, 32)] if s == 0 else weight_block(w, fulls[w], src_t, 3 - g, 0, 32)
+        ok = (z - s >= 0) & (z + 1 < NZ) if d == 0 else (z + s < NZ) & (z - 1 >= 0)
+        dst = weight_block(w, fulls[w], src_t, 3 - g, 0, 32)
+        return ok, remote(src, dst, es.at[w, d, s], er.at[w, d, s], (g, t + 2 * step))
+
+    def extra_wait(w, d, s):
+        blk = weight_block(w, fulls[w], from_t(d, s), 3 - g, 0, 32)
+        remote(blk, blk, es.at[w, d, s], er.at[w, d, s], (g, other)).wait_recv()
+
     def from_t(d, s):
         return t - 2 * (s + 1) if d == 0 else t + 2 * (s + 1)
 
@@ -595,11 +624,11 @@
         remote(blk, blk, sems[0].at[w, d, s], sems[1].at[w, d, s], (gx, t)).wait_recv()
 
     def diag_copy(w, d, s, axis):
-        blk = weight_block(w, fulls[w], from_t(d, s), gx if axis == 0 else gy, axis)
+        blk = weight_block(w, fulls[w], from_t(d, s), gx if axis == 0 else gy, 32 + 32 * axis, 32)
         return remote(blk, blk, ds.at[w, d, s, axis], dr.at[w, d, s, axis], (gy if axis == 0 else gx, t))
 
     def diag_wait(w, d, s, axis):
-        blk = weight_block(w, fulls[w], from_t(d, s), 3 - g, axis)
+        blk = weight_block(w, fulls[w], from_t(d, s), 3 - g, 32 + 32 * axis, 32)
         remote(blk, blk, ds.at[w, d, s, axis], dr.at[w, d, s, axis], (gx, t)).wait_recv()
 
     def core_copy(w, d, s):
@@ -626,9 +655,9 @@
             def _():
                 fn(d)
 
-    def start_z(w, s):
+    def start_z(w, s, kind=None):
         for d in (0, 1):
-            ok, copy = z_copy(w, d, s)
+            ok, copy = (kind or z_copy)(w, d, s)
 
             @pl.when(ok)
             def _():
@@ -647,6 +676,7 @@
         if s == 0 and w < 2:
             start_z(w + 1, 0)
             own_copy(w + 1).start()
+            start_z(w + 1, 0, extra_copy)
 
     def cross(n):
         w, s = divmod(n, 3)
@@ -655,7 +685,10 @@
             for axis in (0, 1):
                 side_wait(w, d, s, axis)
                 diag_copy(w, d, s, axis).start()
+            extra_wait(w, d, s)
         both(s, fn)
+        if s < 2:
+            start_z(w, s + 1, extra_copy)
 
     def finish(n):
         w, s = divmod(n, 3)
@@ -674,12 +707,14 @@
 
     start_z(0, 0)
     own_copy(0).start()
+    start_z(0, 0, extra_copy)
     own_local(0).start()
     local_v = pltpu.make_async_copy(pv, wv.at[t], ls.at[3])
     local_v.start()
     v_copies = [remote(pv, wv.at[t], vs.at[k], vr.at[k], (g, peers[k])) for k in range(7)]
     for copy in v_copies:
         copy.start()
+    to_rows(flat, lin, 2304, 4608)
     for w in (1, 2):
         convert_piece(w, lin, pieces.at[w])
         own_local(w).start()
@@ -736,11 +771,12 @@
         own_copy(w).wait_send()
         for s in range(3):
             for d in (0, 1):
-                ok, copy = z_copy(w, d, s)
-
-                @pl.when(ok)
-                def _():
-                    copy.wait_send()
+                for kind in (z_copy, extra_copy):
+                    ok, copy = kind(w, d, s)
+
+                    @pl.when(ok)
+                    def _():
+                        copy.wait_send()
 
             def sent(d):
                 side_copy(w, d, s, 0).wait_send()
@@ -751,7 +787,7 @@
             both(s, sent)
 
 
-def front(lens, lin, pv, tok):
+def front(lens, master, tok):
     vm = pl.BlockSpec(memory_space=pltpu.VMEM)
     rows = tok.shape[0]
     S = jax.ShapeDtypeStruct
@@ -763,9 +799,12 @@
             S((16, D), F32), S((8, MLP), F32),
             S((rows, D), BF16), S((3, rows, D), BF16), S((rows, D), BF16), S((16, rows), F32),
         ],
-        in_specs=[pl.BlockSpec(memory_space=pltpu.SMEM)] + [vm] * 3,
+        in_specs=[pl.BlockSpec(memory_space=pltpu.SMEM)] + [ANY, vm],
         out_specs=[ANY] * 3 + [vm] * 6,
         scratch_shapes=[
+            pltpu.VMEM((1, master.shape[0]), F32),
+            pltpu.VMEM((6912, 128), F32),
+            pltpu.VMEM((16, 128), F32),
             pltpu.VMEM((3, 4, ROWS, D), BF16),
             pltpu.VMEM((8, 16, 128), F32),
             pltpu.VMEM((3, D, D), BF16),
@@ -774,16 +813,17 @@
             pltpu.VMEM((rows, 128), jnp.int32),
             pltpu.VMEM((rows, D), BF16),
             pltpu.VMEM((rows, 128), F32),
-            DMA((5,)),
+            DMA((6,)),
             DMA((3, 2, 3)), DMA((3, 2, 3)),
             DMA((3, 2, 3)), DMA((3, 2, 3)),
             DMA((3, 2, 3)), DMA((3, 2, 3)),
             DMA((3, 2, 3, 2)), DMA((3, 2, 3, 2)),
             DMA((3, 3, 3)), DMA((3, 3, 3)),
             DMA((7,)), DMA((7,)),
+            DMA((3, 2, 3)), DMA((3, 2, 3)),
         ],
         compiler_params=pltpu.CompilerParams(collective_id=0, has_side_effects=True, vmem_limit_bytes=60 * 2**20),
-    )(lens, lin, pv, tok)
+    )(lens, master, tok)
 
 
 def valid_rows(lens, first, count):
@@ -1113,6 +1153,7 @@
                 run(7 + p, 8 + p)
         weight_grads(normed, proj, gout)
         begin(0)
+        run(12, 14)
         row_grads(column, wide, tall, vec, wa_v, proj, vg)
         store = pltpu.make_async_copy(tall, gin, ls.at[12])
         store.start()
@@ -1121,11 +1162,11 @@
             for j in range(4):
                 lead = 4 * ROWS * k + ROWS * j
                 gv[k, 8 + j : 9 + j, :ROWS] = vg1[0:1, lead : lead + ROWS]
-        run(12, 13)
         for copy in v_copies:
             copy.start()
+        run(14, 15)
         settle(lin, 1)
-        run(13, 18)
+        run(15, 18)
         for k in range(7):
             v_copies[k].wait_recv()
         total = gv[t]
@@ -1135,14 +1176,16 @@
         across = lax.broadcasted_iota(jnp.int32, (16, 128), 0)
         total = jnp.where((lane < ROWS) & (across < 14), total, 0.0)
         sv[...] = total
+
+        def square(i, acc):
+            v = lin[pl.ds(pl.multiple_of(i * 64, 64), 64), :]
+            return acc + v * v
+        acc = lax.fori_loop(36, 108, square, jnp.zeros((64, 128), F32))
         settle(lin, 2)
         lin_store = pltpu.make_async_copy(lin, lin_out, ls.at[13])
         lin_store.start()
 
-        def square(i, acc):
-            v = lin[pl.ds(pl.multiple_of(i * 64, 64), 64), :]
-            return acc + v * v
-        acc = lax.fori_loop(0, 108, square, jnp.zeros((64, 128), F32))
+        acc = lax.fori_loop(0, 36, square, acc)
         qbuf[7] = jnp.full((8, 128), jnp.sum(acc) + jnp.sum(total * total), F32)
         for copy in q_copies:
             copy.start()
@@ -1223,207 +1266,214 @@
 SUM_H, SUM_Q, SUM_E = PARTS // 2, PARTS // 4, PARTS // 8
 MATRIX_WIDTH = PARTS * 128
 VECTOR_WIDTH = 14 * ROWS
-
-
-def finish_kernel(
-    grad, sv, sq, master, first, second, outer,
-    first_new, second_new, mean_out, outer_new, weights_new, vector_out, norm_out,
-    b_master, b_first, b_second, b_outer, b_mean, diff, mean, part, mid, buf, tail_grad, tail, ls, os, ss, rs, ts, tr,
-):
-    g, t, z, c, gx, gy = place()
-    pairs = [(master, b_master.at[0]), (first, b_first), (second, b_second), (outer, b_outer.at[0])]
-    loads = [pltpu.make_async_copy(src, dst, ls.at[i]) for i, (src, dst) in enumerate(pairs)]
-    for copy in loads:
-        copy.start()
-    peers = [gx, gy, 3 - g]
-    barrier = pltpu.get_barrier_semaphore()
-    for peer in peers:
-        pl.semaphore_signal(barrier, inc=1, device_id=(peer, t), device_id_type=MESH_ID)
+BLOCKS = 4
+BLOCK = MATRIX_WIDTH // BLOCKS
+CHUNK = 6144
+
+
+def adam_kernel(grad, sv, sq, master, first, second, first_new, second_new, diff, tail, vector_out, norm_out, tail_grad):
+    i = pl.program_id(0)
     norm = jnp.sqrt(sq[0:1, 0:1])
-    norm_out[...] = jnp.broadcast_to(norm, (8, 128))
     scale = clip_limit / (norm + 1e-06)
-    for j in range(14):
-        tail_grad[0:1, ROWS * j : ROWS * j + ROWS] = sv[j : j + 1, :ROWS]
-    vector_out[...] = tail_grad[...] / jnp.sqrt(F32(8 * 1024))
-    xi, yi = lax.rem(g, 2), lax.div(g, 2)
-    hop = [((gx, t), (gy, t)), ((gy, t), (gx, t))]
-    mine = [(xi, yi), (yi, xi)]
-
-    def line(at):
-        return pl.ds(pl.multiple_of(at.start * 128, 1024), at.size * 128)
-
     step_rate = base_rate * rate_scale
 
-    def adam(value, old_first, old_second, weight, decay):
+    def adam(value, old_first, old_second, weight):
         clipped = value * scale
         new_first = beta_first * old_first + (1.0 - beta_first) * clipped
         new_second = beta_second * old_second + (1.0 - beta_second) * clipped * clipped
         root = jnp.sqrt(new_second * (1.0 / (1.0 - beta_second**adam_count))) + adam_epsilon
         ahead = new_first * (1.0 / (1.0 - beta_first**adam_count)) / root
-        if decay:
+        if weight is not None:
             ahead = ahead + weight_decay * weight
         return new_first, new_second, step_rate * ahead
 
-    def nesterov(weight, momentum, average):
-        new_momentum = outer_beta * momentum + average
-        return new_momentum, weight - outer_rate * (average + outer_beta * new_momentum)
-
-    def rows_loop(lo, count, fn):
-        chunk = 48
-
+    @pl.when(i < BLOCKS)
+    def _():
+        def body(n, _):
+            flat = pl.ds(pl.multiple_of(n * CHUNK, CHUNK), CHUNK)
+            at = pl.ds(pl.multiple_of(n * (CHUNK // 128), CHUNK // 128), CHUNK // 128)
+            first_new[:, flat], second_new[:, flat], ahead = adam(
+                grad[at, :].reshape(1, CHUNK), first[:, flat], second[:, flat], master[flat].reshape(1, CHUNK)
+            )
+            diff[at, :] = ahead.reshape(CHUNK // 128, 128).astype(BF16)
+            return 0
+        lax.fori_loop(0, BLOCK // CHUNK, body, 0, unroll=12)
+
+    @pl.when(i == BLOCKS)
+    def _():
+        norm_out[...] = jnp.broadcast_to(norm, (8, 128))
+        for j in range(14):
+            tail_grad[0:1, ROWS * j : ROWS * j + ROWS] = sv[j : j + 1, :ROWS]
+        vector_out[...] = tail_grad[...] / jnp.sqrt(F32(8 * 1024))
+        at = pl.ds(0, VECTOR_WIDTH)
+        first_new[:, at], second_new[:, at], ahead = adam(tail_grad[...], first[:, at], second[:, at], None)
+        tail[...] = jnp.zeros_like(tail)
+        tail[:, at] = ahead
+
+
+def adam_step(grad, sv, sq, master, first, second):
+    S = jax.ShapeDtypeStruct
+    n = master.shape[0]
+
+    def whole(shape):
+        return pl.BlockSpec(shape, lambda i: (0, 0))
+
+    line = pl.BlockSpec((1, BLOCK), lambda i: (0, i))
+    rows = pl.BlockSpec((PARTS // BLOCKS, 128), lambda i: (jnp.minimum(i, BLOCKS - 1), 0))
+    return pl.pallas_call(
+        adam_kernel,
+        name="adam",
+        grid=(BLOCKS + 1,),
+        out_shape=[
+            S((1, n), F32), S((1, n), F32), S((PARTS, 128), BF16), S((1, 1408), F32), S((1, VECTOR_WIDTH), F32), S((8, 128), F32)
+        ],
+        in_specs=[rows, whole((16, 128)), whole((8, 128)), pl.BlockSpec((BLOCK,), lambda i: (i,)), line, line],
+        out_specs=[line, line, rows, whole((1, 1408)), whole((1, VECTOR_WIDTH)), whole((8, 128))],
+        scratch_shapes=[pltpu.VMEM((1, VECTOR_WIDTH), F32)],
+    )(grad, sv, sq, master, first, second)
+
+
+def outer_kernel(mean, tail, master, momentum, mean_out, momentum_out, weights_out):
+    i = pl.program_id(0)
+
+    def step(flat, average):
+        new_momentum = outer_beta * momentum[flat] + average
+        mean_out[flat] = average
+        momentum_out[flat] = new_momentum
+        weights_out[flat] = master[flat] - outer_rate * (average + outer_beta * new_momentum)
+
+    @pl.when(i < BLOCKS)
+    def _():
+        def body(n, _):
+            flat = pl.ds(pl.multiple_of(n * CHUNK, CHUNK), CHUNK)
+            at = pl.ds(pl.multiple_of(n * (CHUNK // 128), CHUNK // 128), CHUNK // 128)
+            step(flat, mean[at, :].astype(F32).reshape(CHUNK))
+            return 0
+        lax.fori_loop(0, BLOCK // CHUNK, body, 0, unroll=12)
+
+    @pl.when(i == BLOCKS)
+    def _():
+        step(pl.ds(0, 1408), tail[0, :])
+
+
+def outer_step(mean, tail, master, momentum):
+    n = master.shape[0]
+    line = pl.BlockSpec((BLOCK,), lambda i: (i,))
+    return pl.pallas_call(
+        outer_kernel,
+        name="outer",
+        grid=(BLOCKS + 1,),
+        out_shape=[jax.ShapeDtypeStruct((n,), F32)] * 3,
+        in_specs=[
+            pl.BlockSpec((PARTS // BLOCKS, 128), lambda i: (jnp.minimum(i, BLOCKS - 1), 0)),
+            pl.BlockSpec((1, 1408), lambda i: (0, 0)), line, line,
+        ],
+        out_specs=[line] * 3,
+    )(mean, tail, master, momentum)
+
+
+def mean_kernel(diff, tail, mean, tail_mean, part, mid, buf, tails, ss, rs, ts, tr):
+    g, t, z, c, gx, gy = place()
+    peers = [gx, gy, 3 - g]
+    greet([(peer, t) for peer in peers], 3)
+    xi, yi = lax.rem(g, 2), lax.div(g, 2)
+    hop = [((gx, t), (gy, t)), ((gy, t), (gx, t))]
+    mine = [(xi, yi), (yi, xi)]
+
+    def at(h, i, j):
+        return h * SUM_H + i * SUM_Q + j * SUM_E
+
+    def to_sum(h, e):
+        a, b = mine[h]
+        j = 1 - b if e == 0 else b
+        src = rows_at(diff, at(h, 1 - a, j), SUM_E)
+        return remote(src, part.at[h, e], ss.at[h, e], rs.at[h, e], hop[h][0])
+
+    def over(h):
+        return remote(mid.at[h], buf.at[h], ss.at[h, 2], rs.at[h, 2], hop[h][1])
+
+    def share(h, e):
+        a, b = mine[h]
+        block = rows_at(mean, at(h, a, 1 - b if e == 2 else b), SUM_E)
+        return remote(block, block, ss.at[h, 3 + e], rs.at[h, 3 + e], hop[h][1 if e == 0 else 0])
+
+    def landed(h, e):
+        a, b = mine[h]
+        block = rows_at(mean, at(h, a, 1 - b) if e == 0 else at(h, 1 - a, 1 - b if e == 2 else b), SUM_E)
+        remote(block, block, ss.at[h, 3 + e], rs.at[h, 3 + e], hop[h][0]).wait_recv()
+
+    def add(fn):
         def body(i, _):
-            fn(pl.ds(pl.multiple_of(lo + i * chunk, 16), chunk), pl.ds(pl.multiple_of(i * chunk, 16), chunk))
+            fn(pl.multiple_of(i * 96, 96))
             return 0
-        lax.fori_loop(0, count // chunk, body, 0)
-
-    def adam_rows(lo, count):
-        def fn(at, _):
-            flat = line(at)
-            b_first[:, flat], b_second[:, flat], ahead = adam(
-                grad[at, :].reshape(1, -1), b_first[:, flat], b_second[:, flat], b_master[:, flat], True
-            )
-            diff[at, :] = ahead.reshape(-1, 128).astype(BF16)
-        rows_loop(lo, count, fn)
-
-    def outer_rows(lo, count):
-        def fn(at, _):
-            flat = line(at)
-            average = mean[at, :].astype(F32).reshape(1, -1)
-            b_mean[:, flat] = average
-            b_outer[:, flat], b_master[:, flat] = nesterov(b_master[:, flat], b_outer[:, flat], average)
-        rows_loop(lo, count, fn)
-
-    def copies(h):
-        a, b = mine[h]
-        base = h * SUM_H
-        sent = rows_at(diff, base + (1 - a) * SUM_Q, SUM_Q)
-        one = remote(sent, part.at[h], ss.at[h, 0], rs.at[h, 0], hop[h][0])
-        two = remote(rows_at(mid.at[h], (1 - b) * SUM_E, SUM_E), buf.at[h], ss.at[h, 1], rs.at[h, 1], hop[h][1])
-        done = rows_at(mean, base + a * SUM_Q + b * SUM_E, SUM_E)
-        three = remote(done, done, ss.at[h, 2], rs.at[h, 2], hop[h][1])
-        whole = rows_at(mean, base + a * SUM_Q, SUM_Q)
-        four = remote(whole, whole, ss.at[h, 3], rs.at[h, 3], hop[h][0])
-        return one, two, three, four
-
-    steps = [copies(0), copies(1)]
-    for copy in loads[:3]:
-        copy.wait()
-    for h in (0, 1):
-        adam_rows(h * SUM_H + (1 - mine[h][0]) * SUM_Q, SUM_Q)
-        if h == 0:
-            pl.semaphore_wait(barrier, 3)
-        steps[h][0].start()
-    at_tail = pl.ds(MATRIX_WIDTH, VECTOR_WIDTH)
-    new_first, new_second, ahead = adam(tail_grad[...], b_first[:, at_tail], b_second[:, at_tail], None, False)
-    b_first[:, at_tail] = new_first
-    b_second[:, at_tail] = new_second
-    tail[3, :, :] = jnp.zeros((1, 1408), F32)
-    tail[3, :, pl.ds(0, VECTOR_WIDTH)] = ahead
-    t_copies = [remote(tail.at[3], tail.at[k], ts.at[k], tr.at[k], (peers[k], t)) for k in range(3)]
+        lax.fori_loop(0, SUM_E // 96, body, 0)
+
+    for e in (0, 1):
+        for h in (0, 1):
+            to_sum(h, e).start()
+    t_copies = [remote(tail, tails.at[k], ts.at[k], tr.at[k], (peers[k], t)) for k in range(3)]
     for copy in t_copies:
         copy.start()
     for h in (0, 1):
-        adam_rows(h * SUM_H + mine[h][0] * SUM_Q, SUM_Q)
-    stores = [pltpu.make_async_copy(b_first, first_new, os.at[0]), pltpu.make_async_copy(b_second, second_new, os.at[1])]
-    for copy in stores:
-        copy.start()
+        a, b = mine[h]
+        to_sum(h, 0).wait_recv()
+
+        def first(i):
+            total = diff[pl.ds(pl.multiple_of(at(h, a, 1 - b) + i, 32), 96), :].astype(F32)
+            mid[h, pl.ds(i, 96), :] = (total + part[h, 0, pl.ds(i, 96), :].astype(F32)).astype(BF16)
+        add(first)
+        over(h).start()
     for h in (0, 1):
         a, b = mine[h]
-        steps[h][0].wait_recv()
-        lo = (1 - b) * SUM_E
-        src = h * SUM_H + a * SUM_Q + lo
-
-        def fn(at, local):
-            here = pl.ds(pl.multiple_of(lo + local.start, 16), local.size)
-            mid[h, here, :] = (diff[at, :].astype(F32) + part[h, here, :].astype(F32)).astype(BF16)
-        rows_loop(src, SUM_E, fn)
-        steps[h][1].start()
-    loads[3].wait()
-    for h in (0, 1):
-        a, b = mine[h]
-        steps[h][1].wait_recv()
-        lo = b * SUM_E
-        src = h * SUM_H + a * SUM_Q + lo
-
-        def fn(at, local):
-            here = pl.ds(pl.multiple_of(lo + local.start, 16), local.size)
-            total = diff[at, :].astype(F32) + part[h, here, :].astype(F32) + buf[h, local, :].astype(F32)
-            mean[at, :] = (total * 0.25).astype(BF16)
-        rows_loop(src, SUM_E, fn)
-        steps[h][2].start()
+        to_sum(h, 1).wait_recv()
+        over(h).wait_recv()
+
+        def second(i):
+            here = pl.ds(pl.multiple_of(at(h, a, b) + i, 32), 96)
+            local = pl.ds(i, 96)
+            total = diff[here, :].astype(F32) + part[h, 1, local, :].astype(F32) + buf[h, local, :].astype(F32)
+            mean[here, :] = (total * 0.25).astype(BF16)
+        add(second)
+        share(h, 0).start()
+        share(h, 1).start()
     for copy in t_copies:
         copy.wait_recv()
-    total = tail[3] + tail[0] + tail[1] + tail[2]
-    average = total[:, :VECTOR_WIDTH] * 0.25
-    b_mean[:, at_tail] = average
-    new_momentum, new_weights = nesterov(b_master[:, at_tail], b_outer[:, at_tail], average)
-    b_outer[:, at_tail] = new_momentum
-    b_master[:, at_tail] = new_weights
+    tail_mean[...] = (tail[...] + tails[0] + tails[1] + tails[2]) * 0.25
     for h in (0, 1):
-        a, b = mine[h]
-        outer_rows(h * SUM_H + a * SUM_Q + b * SUM_E, SUM_E)
+        landed(h, 0)
+        share(h, 2).start()
     for h in (0, 1):
-        a, b = mine[h]
-        rest = h * SUM_H + a * SUM_Q + (1 - b) * SUM_E
-        other = rows_at(mean, rest, SUM_E)
-        remote(other, other, ss.at[h, 2], rs.at[h, 2], hop[h][1]).wait_recv()
-        steps[h][2].wait_send()
-        steps[h][3].start()
-        outer_rows(rest, SUM_E)
-    for h in (0, 1):
-        a, b = mine[h]
-        rest = h * SUM_H + (1 - a) * SUM_Q
-        other = rows_at(mean, rest, SUM_Q)
-        remote(other, other, ss.at[h, 3], rs.at[h, 3], hop[h][0]).wait_recv()
-        outer_rows(rest, SUM_Q)
-    last = [
-        pltpu.make_async_copy(b_mean.at[0], mean_out, os.at[2]),
-        pltpu.make_async_copy(b_outer.at[0], outer_new, os.at[3]),
-        pltpu.make_async_copy(b_master.at[0], weights_new, os.at[4]),
-    ]
-    for copy in last:
-        copy.start()
-    for h in (0, 1):
-        steps[h][0].wait_send()
-        steps[h][1].wait_send()
-        steps[h][3].wait_send()
+        landed(h, 1)
+        landed(h, 2)
+        for e in (0, 1):
+            to_sum(h, e).wait_send()
+        over(h).wait_send()
+        for e in range(3):
+            share(h, e).wait_send()
     for copy in t_copies:
         copy.wait_send()
-    for copy in stores + last:
-        copy.wait()
-
-
-def finish(grad, sv, sq, master, first, second, outer):
+
+
+def mean_groups(diff, tail):
     vm = pl.BlockSpec(memory_space=pltpu.VMEM)
     S = jax.ShapeDtypeStruct
-    n = master.shape[0]
-    flat = pltpu.VMEM((1, n), F32)
+    V = pltpu.VMEM
     return pl.pallas_call(
-        finish_kernel,
-        name="finish",
-        out_shape=[S((1, n), F32)] * 2 + [S((n,), F32)] * 3 + [S((1, VECTOR_WIDTH), F32), S((8, 128), F32)],
-        in_specs=[vm] * 3 + [ANY] * 4,
-        out_specs=[ANY] * 5 + [vm] * 2,
-        scratch_shapes=[flat] * 5
-        + [
-            pltpu.VMEM((PARTS, 128), BF16),
-            pltpu.VMEM((PARTS, 128), BF16),
-            pltpu.VMEM((2, SUM_Q, 128), BF16),
-            pltpu.VMEM((2, SUM_Q, 128), BF16),
-            pltpu.VMEM((2, SUM_E, 128), BF16),
-            pltpu.VMEM((1, VECTOR_WIDTH), F32),
-            pltpu.VMEM((4, 1, 1408), F32),
-            DMA((4,)), DMA((5,)), DMA((2, 4)), DMA((2, 4)), DMA((3,)), DMA((3,)),
+        mean_kernel,
+        name="mean_groups",
+        out_shape=[S((PARTS, 128), BF16), S((1, 1408), F32)],
+        in_specs=[vm] * 2,
+        out_specs=[vm] * 2,
+        scratch_shapes=[
+            V((2, 2, SUM_E, 128), BF16), V((2, SUM_E, 128), BF16), V((2, SUM_E, 128), BF16), V((3, 1, 1408), F32),
+            DMA((2, 6)), DMA((2, 6)), DMA((3,)), DMA((3,)),
         ],
-        compiler_params=pltpu.CompilerParams(collective_id=2, has_side_effects=True, vmem_limit_bytes=60 * 2**20),
-    )(grad, sv, sq, master, first, second, outer)
+        compiler_params=pltpu.CompilerParams(collective_id=2, has_side_effects=True),
+    )(diff, tail)
 
 
 def on_small_slice(tokens, cotangent, crop_lengths, master, first_moment, second_moment, outer_momentum):
-    lin = master[:MATRIX_WIDTH].reshape(-1, 128)
-    vector = master[MATRIX_WIDTH:].astype(BF16).astype(F32).reshape(14, ROWS)
-    piece = jnp.pad(vector, ((0, 2), (0, 128 - ROWS)))
-    wa, wb, wc, vec, fb1, normed, projected, attended, lse = front(crop_lengths, lin, piece, tokens)
+    wa, wb, wc, vec, fb1, normed, projected, attended, lse = front(crop_lengths, master, tokens)
     block_output, slope, normed_two, grad_fc2, vg = forward(
         crop_lengths, tokens, cotangent, attended, wa, wb, wc.reshape(MLP, D), vec, fb1
     )
@@ -1431,9 +1481,11 @@
         crop_lengths, vec, vg, tokens, cotangent, wa, wb, wc.reshape(MLP, D), attended, slope, normed_two, normed,
         projected, lse, grad_fc2
     )
-    moment_one, moment_two, mean_difference, outer_new, new_weights, vector_part, norm = finish(
-        grad_lin, sv, sq, master, first_moment, second_moment, outer_momentum
+    moment_one, moment_two, difference, tail, vector_part, norm = adam_step(
+        grad_lin, sv, sq, master, first_moment, second_moment
     )
+    mean, tail_mean = mean_groups(difference, tail)
+    mean_difference, outer_new, new_weights = outer_step(mean, tail_mean, master, outer_momentum)
     return (
         block_output,
         input_grad,

time: 336 us -> 308 us (0.917)
  local copies, waits for them, and re-layouts: 23.6 us -> 2.87 us
  Pallas kernels: 307 us -> 300 us
    unnamed x21 -> x3, local copies, waits for them, and re-layouts: 17.4 us -> 1.67 us
    pallas_call x1, Pallas kernels: 141 us -> 132 us  [back(): pl.pallas_call(back_kernel, name='back', out_shape=[S((rows, D), F32), S(...]
    reshape x1 -> x0, local copies, waits for them, and re-layouts: 4.02 us -> none  [on_small_slice(): lin = master[:MATRIX_WIDTH].reshape(-1, 128)]
    pallas_call x1 -> x3, Pallas kernels: 52.7 us -> 56.3 us  [the longest x1 37.8 us: mean_groups(): pl.pallas_call(mean_kernel, name='mean_groups', out_shape=[S((PARTS, 128)...]
where the time goes in v1:
time: 308 us; the launch traced here: 304 us
  Pallas kernels  300 us (97%)
    pallas_call x1, Pallas kernels, back(): pl.pallas_call(back_kernel, name='back', out_shape=[S((rows, D), F32), S(...  132 us
    pallas_call x1, Pallas kernels, front(): pl.pallas_call(front_kernel, name='front', out_shape=[S((4, D, D), BF16),...  78.6 us
    pallas_call x1, Pallas kernels, mean_groups(): pl.pallas_call(mean_kernel, name='mean_groups', out_shape=[S((PARTS, 128)...  37.8 us
    pallas_call x1, Pallas kernels, forward(): pl.pallas_call(forward_kernel, name='mlp_forward', out_shape=[S((rows, D)...  33.1 us
    pallas_call x1, Pallas kernels, adam_step(): pl.pallas_call(adam_kernel, name='adam', grid=(BLOCKS + 1,), out_shape=[S...  10.1 us
    pallas_call x1, Pallas kernels, outer_step(): pl.pallas_call(outer_kernel, name='outer', grid=(BLOCKS + 1,), out_shape=...  8.54 us

profile of v1, /device:TPU:0, one launch (start us, length us, event | category | flops | bytes accessed | tf_op | source)
XLA Modules:
  0.0 304.0 jit_solution(13959678195924266446)
XLA Ops:
  0.6 78.6 %front.1 = (bf16[4,768,768]{2,1,0:T(8,128)(2,1)}, bf16[4,768,768]{2,1,0:T(8,128)(2,1)}, bf16[8,4,96,768]{3,2,1,0:T(8,128)(2,1)}, f32[16,768]{1,0:T(8,128)}, f32[...) custom-call(s32[1,10]{1,0:T(1,128)} %lens.5, ...), custom_call_target="tpu_custom_call" | custom-call | tf_op jit(solution)/shard_map/front/pallas_call | solution.py:794
  79.3 33.1 %mlp_forward.1 = (f32[1024,768]{1,0:T(8,128)}, bf16[1024,3072]{1,0:T(8,128)(2,1)}, bf16[1024,768]{1,0:T(8,128)(2,1)}, bf16[8,4,96,768]{3,2,1,0:T(8,128)(2,1)}, f32[16,768]{1,0:T(8,128)}) custom-call(s32[1,10]{1,0:T(1,128)} %lens.5, f32[1024,768]{1,0:T(8,128)} %tok.3, f32[1024,768]{1,0:T(8,128)} %cot.1, bf16[1024,768]{1,0:T(8,128)(2,1)} %get-tuple-element.38.att_in, ...), custom_call_target="tpu_custom_call" | custom-call | tf_op jit(solution)/shard_map/mlp_forward/pallas_call | solution.py:907
  112.4 132.1 %back.1 = (f32[1024,768]{1,0:T(8,128)}, f32[6912,128]{1,0:T(8,128)}, f32[16,128]{1,0:T(8,128)}, f32[8,128]{1,0:T(8,128)}) custom-call(s32[1,10]{1,0:T(1,128)} %lens.5, f32[16,768]{1,0:T(8,128)} %get-tuple-element.42.vec, f32[16,768]{1,0:T(8,128)} %get-tuple-element.45.vg_in, f32[1024,768]{1,0:T(8,128)} %tok.3, f32[1024,768]{1,0:T(8,128)} %cot.1, ...), custom_call_target="tpu_custom_call" | custom-call | tf_op jit(solution)/shard_map/back/pallas_call | solution.py:1233
  244.5 10.1 %adam.1 = (f32[1,886080]{1,0:T(1,128)}, f32[1,886080]{1,0:T(1,128)}, bf16[6912,128]{1,0:T(8,128)(2,1)}, f32[1,1408]{1,0:T(1,128)}, f32[1,1344]{1,0:T(1,128)}, /*index=5*/f32[8,128]{1,0:T(8,128)}) custom-call(f32[6912,128]{1,0:T(8,128)} %get-tuple-element.53.grad, f32[16,128]{1,0:T(8,128)} %get-tuple-element.54.sv, f32[8,128]{1,0:T(8,128)} %get-tuple-element.55.sq, ...), custom_call_target="tpu_custom_call" | custom-call | tf_op jit(solution)/shard_map/adam/pallas_call | solution.py:1323
  254.6 1.2 slice.3
  255.8 37.8 %mean_groups.1 = (bf16[6912,128]{1,0:T(8,128)(2,1)}, f32[1,1408]{1,0:T(1,128)}) custom-call(bf16[6912,128]{1,0:T(8,128)(2,1)} %get-tuple-element.60.diff, f32[1,1408]{1,0:T(1,128)} %get-tuple-element.61.tail), custom_call_target="tpu_custom_call" | custom-call | tf_op jit(solution)/shard_map/mean_groups/pallas_call | solution.py:1461
  293.5 0.0 copy-start
  293.5 8.5 %outer.1 = (f32[886080]{0:T(1024)}, f32[886080]{0:T(1024)}, f32[886080]{0:T(1024)}) custom-call(bf16[6912,128]{1,0:T(8,128)(2,1)} %get-tuple-element.62.mean, f32[1,1408]{1,0:T(1,128)} %get-tuple-element.63.tail, f32[886080]{0:T(1024)} %master.5, f32[886080]{0:T(1024)} %momentum.1), custom_call_target="tpu_custom_call" | custom-call | tf_op jit(solution)/shard_map/outer/pallas_call | solution.py:1362
  302.1 0.0 copy-done
  302.1 1.7 copy.17
Async XLA Ops:
  293.5 8.5 %copy-start = (f32[1024,768]{1,0:T(8,128)S(1)}, f32[1024,768]{1,0:T(8,128)}, u32[]{:S(2)}) copy-start(f32[1024,768]{1,0:T(8,128)} %get-tuple-element.77) | copy-start | bytes 9437188

commit v2 on v1

--- a/solution.py
+++ b/solution.py
@@ -305,7 +305,7 @@
     return ref.at[pl.ds(pl.multiple_of(start, 16), count), :]
 
 
-TILE = 256
+TILE = 512
 
 
 def nn(a, b):
@@ -836,8 +836,8 @@
 
 def forward_kernel(
     lens, tok_in, cot_in, att_in, wa, wb_in, wc_in, vec, fb1,
-    bo_out, slope_out, n2_out, gc_out, vg,
-    tok, cot, att, wp, wb, wc, bo, slope, n2, hid, gb2, gc, ls, os,
+    bo_out, slope_out, n2_out, hid_out, vg,
+    tok, cot, att, wp, wb, wc, bo, slope, n2, hid, ls, os,
 ):
     pairs = [(att_in, att), (wa.at[3], wp), (tok_in, tok), (wb_in, wb), (wc_in, wc), (cot_in, cot)]
     loads = [pltpu.make_async_copy(src, dst, ls.at[i]) for i, (src, dst) in enumerate(pairs)]
@@ -851,7 +851,7 @@
 
     def stores(i):
         at = pl.ds(i * TILE, TILE)
-        trio = [(bo, bo_out), (slope, slope_out), (n2, n2_out)]
+        trio = [(slope, slope_out), (n2, n2_out), (hid, hid_out), (bo, bo_out)]
         return [pltpu.make_async_copy(a.at[at, :], b.at[at, :], os.at[i, n]) for n, (a, b) in enumerate(trio)]
 
     for copy in loads[:3]:
@@ -876,27 +876,18 @@
         if i == 0:
             loads[4].wait()
             loads[5].wait()
+        for copy in stores(i)[:3]:
+            copy.start()
         branch_two = nn(hid[at, :], wc[...]) + row(12)
         bo[at, :] += row(13) * branch_two
         back = cot[at, :] * valid_rows(lens, i * TILE, TILE)
         low_back = (row(13) * back).astype(BF16)
-        gb2[at, :] = low_back
         vg[13:14, :] += col_sum(back * branch_two)
         vg[12:13, :] += col_sum(low_back.astype(F32))
-        for copy in stores(i):
-            copy.start()
-
-    def fc2(t, _):
-        low = pl.ds(pl.multiple_of(t * 384, 128), 384)
-        gc[t] = tn(hid[:, low], gb2[...]).astype(BF16).reshape(4, ROWS, D)
-        return 0
-    lax.fori_loop(0, 8, fc2, 0)
-    store = pltpu.make_async_copy(gc, gc_out, os.at[4, 0])
-    store.start()
+        stores(i)[3].start()
     for i in range(rows // TILE):
         for copy in stores(i):
             copy.wait()
-    store.wait()
 
 
 def forward(lens, tok, cot, att, wa, wb, wc, vec, fb1):
@@ -907,27 +898,28 @@
     return pl.pallas_call(
         forward_kernel,
         name="mlp_forward",
-        out_shape=[S((rows, D), F32), S((rows, MLP), BF16), S((rows, D), BF16), S((8, 4, ROWS, D), BF16), S((16, D), F32)],
+        out_shape=[S((rows, D), F32), S((rows, MLP), BF16), S((rows, D), BF16), S((rows, MLP), BF16), S((16, D), F32)],
         in_specs=[pl.BlockSpec(memory_space=pltpu.SMEM)] + [ANY] * 6 + [vm] * 2,
         out_specs=[ANY] * 4 + [vm],
         scratch_shapes=[
             V((rows, D), F32), V((rows, D), F32), V((rows, D), BF16), V((D, D), BF16),
             V((4, D, D), BF16), V((MLP, D), BF16), V((rows, D), F32), V((rows, MLP), BF16),
-            V((rows, D), BF16), V((rows, MLP), BF16), V((rows, D), BF16), V((8, 4, ROWS, D), BF16),
-            DMA((6,)), DMA((5, 3)),
+            V((rows, D), BF16), V((rows, MLP), BF16),
+            DMA((6,)), DMA((4, 4)),
         ],
         compiler_params=pltpu.CompilerParams(vmem_limit_bytes=62 * 2**20),
     )(lens, tok, cot, att, wa, wb, wc, vec, fb1)
 
 
 ORDER = (2, 1, 0)
+FIRST = (3, 0, 2, 1)
 
 
 def back_kernel(
-    lens, vec, vg_in, tok, cot, wa, wb_in, wc_in, att_in, slope_in, n2_in, normed_in, proj_in, lse_in, gc,
+    lens, vec, vg_in, tok, cot, wa, wb_in, wc_in, att_in, slope_in, hid_in, n2_in, normed_in, proj_in, lse_in,
     gin, lin_out, sv, sq,
     line, column, wide, tall, gatt, gout, gb, own, core, zbuf, vg, vg1, gv, vbuf, qbuf,
-    ls, os, cs, cr, zs, zr, vs, vr, qs, qr,
+    ls, hs, cs, cr, zs, zr, vs, vr, qs, qr,
 ):
     g, t, z, c, gx, gy = place()
     peers = [lax.rem(t + k, 8) for k in range(1, 8)]
@@ -943,19 +935,14 @@
     greet([(g, p) for p in peers], 7)
 
     def own_at(w, k):
-        return (gout.at[2 * k + c], gb.at[2 * k + c], own.at[k])[w]
+        return own.at[k] if w == 2 else (gout, gb)[w].at[2 * k + c]
 
     def core_copy(w, k):
-        return remote((gout, gb, gc)[w].at[2 * k + 1 - c], core.at[w, k], cs.at[w, k], cr.at[w, k], (g, other))
-
-    def load(k):
-        return pltpu.make_async_copy(gc.at[2 * k + c], own.at[k], os.at[k])
+        return remote((gout, gb, gout)[w].at[2 * k + 1 - c], core.at[w, k], cs.at[w, k], cr.at[w, k], (g, other))
 
     def begin(w):
-        for k in (3, 0, 2, 1):
+        for k in FIRST:
             core_copy(w, k).start()
-            if w == 2:
-                load(k).start()
 
     def slot(d, k, to):
         return k - to if d == 0 else 4 - (to - k)
@@ -1008,8 +995,6 @@
         remote(here, here, zs.at[w, d, k, h], zr.at[w, d, k, h], (g, other)).wait_recv()
 
     def ready(w, k):
-        if w == 2:
-            load(k).wait()
         core_copy(w, k).wait_recv()
 
     def pass_on(i, d, j, h):
@@ -1060,30 +1045,54 @@
             pass_on(i, 0, j, h)
             pass_on(i, 1, j, h)
 
-    begin(2)
     find_places(lens, line, column)
     vg[...] = vg_in[...]
     vg1[...] = jnp.zeros_like(vg1)
 
     def mlp_part(wp, wb, wc, grads, n2, att, gb1):
-        inner = local(
-            [(att_in, att), (wa.at[3], wp), (wc_in, wc), (slope_in, grads), (wb_in, wb), (n2_in, n2)], 2
-        )
+        inner = local([(att_in, att), (wa.at[3], wp), (wc_in, wc), (wb_in, wb), (n2_in, n2)], 2)
+
+        def hidden_load(q):
+            low = pl.ds(q * D, D)
+            return pltpu.make_async_copy(hid_in.at[:, low], grads.at[:, low], hs.at[q])
+
+        def slope_load(i):
+            at = pl.ds(i * TILE, TILE)
+            return pltpu.make_async_copy(slope_in.at[at, :], grads.at[at, :], hs.at[4 + i])
+
+        for q in FIRST:
+            hidden_load(q).start()
         for copy in inner:
             copy.start()
-        run(0, 2)
-        for copy in loads + inner:
-            copy.wait()
 
         def row(j):
             return vec[j : j + 1, :]
 
+        for copy in loads:
+            copy.wait()
+        for i in range(rows // TILE):
+            at = pl.ds(i * TILE, TILE)
+            tall[at, :] = tall[at, :] * valid_rows(lens, i * TILE, TILE)
+            gb1[at, :] = (row(13) * tall[at, :]).astype(BF16)
+        for q in FIRST:
+            hidden_load(q).wait()
+
+            for t_at, dst in ((2 * q + 1 - c, gout.at[2 * q + 1 - c]), (2 * q + c, own.at[q])):
+                low = pl.ds(pl.multiple_of(t_at * 384, 128), 384)
+                dst[...] = tn(grads[:, low], gb1[...]).astype(BF16).reshape(4, ROWS, D)
+            core_copy(2, q).start()
+        for i in range(rows // TILE):
+            slope_load(i).start()
+        run(0, 2)
+        for copy in inner:
+            copy.wait()
+
         def tile(i):
             at = pl.ds(i * TILE, TILE)
+            slope_load(i).wait()
             branch_one = nn(att[at, :], wp[...]) + row(4)
             normal, inverse = normalize(wide[at, :] + row(5) * branch_one)
-            tall[at, :] = tall[at, :] * valid_rows(lens, i * TILE, TILE)
-            low_back = (row(13) * tall[at, :]).astype(BF16)
+            low_back = gb1[at, :]
 
             def backward(q, total):
                 low = pl.ds(pl.multiple_of(q * D, D), D)
@@ -1105,7 +1114,7 @@
 
         for i in range(rows // TILE):
             tile(i)
-            run(2 + i, 3 + i)
+            run(2 + 2 * i, 4 + 2 * i)
 
         def fc1(q, _):
             def part(m, _):
@@ -1116,6 +1125,9 @@
             return lax.fori_loop(0, 2, part, 0)
         lax.fori_loop(0, 4, fc1, 0)
         begin(1)
+
+        for q in FIRST:
+            core_copy(2, q).wait_send()
 
         def proj_part(m, _):
             col = pl.ds(pl.multiple_of(m * 384, 128), 384)
@@ -1203,7 +1215,7 @@
         pltpu.VMEM((rows, D), BF16),
         pltpu.VMEM((3, rows, D), BF16),
     )
-    for w in range(3):
+    for w in range(2):
         for k in range(NZ):
             core_copy(w, k).wait_send()
     for h in (0, 1):
@@ -1225,7 +1237,7 @@
         v_copies[k].wait_send()
 
 
-def back(lens, vec, vg, tok, cot, wa, wb, wc, att, slope, n2, normed, proj, lse_t, gc):
+def back(lens, vec, vg, tok, cot, wa, wb, wc, att, slope, hid, n2, normed, proj, lse_t):
     vm = pl.BlockSpec(memory_space=pltpu.VMEM)
     rows = tok.shape[0]
     S = jax.ShapeDtypeStruct
@@ -1252,14 +1264,14 @@
             V((8, 16, 128), F32),
             V((7, 16, 128), F32),
             V((8, 8, 128), F32),
-            DMA((14,)), DMA((NZ,)), DMA((3, NZ)), DMA((3, NZ)),
+            DMA((14,)), DMA((8,)), DMA((3, NZ)), DMA((3, NZ)),
             DMA((3, 2, NZ, 2)), DMA((3, 2, NZ, 2)),
             DMA((7,)), DMA((7,)), DMA((7,)), DMA((7,)),
         ],
         compiler_params=pltpu.CompilerParams(
             collective_id=1, has_side_effects=True, vmem_limit_bytes=63 * 2**20
         ),
-    )(lens, vec, vg, tok, cot, wa, wb, wc, att, slope, n2, normed, proj, lse_t, gc)
+    )(lens, vec, vg, tok, cot, wa, wb, wc, att, slope, hid, n2, normed, proj, lse_t)
 
 
 PARTS = 6912
@@ -1301,7 +1313,7 @@
 
     @pl.when(i == BLOCKS)
     def _():
-        norm_out[...] = jnp.broadcast_to(norm, (8, 128))
+        norm_out[...] = norm
         for j in range(14):
             tail_grad[0:1, ROWS * j : ROWS * j + ROWS] = sv[j : j + 1, :ROWS]
         vector_out[...] = tail_grad[...] / jnp.sqrt(F32(8 * 1024))
@@ -1325,10 +1337,10 @@
         name="adam",
         grid=(BLOCKS + 1,),
         out_shape=[
-            S((1, n), F32), S((1, n), F32), S((PARTS, 128), BF16), S((1, 1408), F32), S((1, VECTOR_WIDTH), F32), S((8, 128), F32)
+            S((1, n), F32), S((1, n), F32), S((PARTS, 128), BF16), S((1, 1408), F32), S((1, VECTOR_WIDTH), F32), S((1, 1), F32)
         ],
         in_specs=[rows, whole((16, 128)), whole((8, 128)), pl.BlockSpec((BLOCK,), lambda i: (i,)), line, line],
-        out_specs=[line, line, rows, whole((1, 1408)), whole((1, VECTOR_WIDTH)), whole((8, 128))],
+        out_specs=[line, line, rows, whole((1, 1408)), whole((1, VECTOR_WIDTH)), whole((1, 1))],
         scratch_shapes=[pltpu.VMEM((1, VECTOR_WIDTH), F32)],
     )(grad, sv, sq, master, first, second)
 
@@ -1474,12 +1486,12 @@
 
 def on_small_slice(tokens, cotangent, crop_lengths, master, first_moment, second_moment, outer_momentum):
     wa, wb, wc, vec, fb1, normed, projected, attended, lse = front(crop_lengths, master, tokens)
-    block_output, slope, normed_two, grad_fc2, vg = forward(
+    block_output, slope, normed_two, hidden, vg = forward(
         crop_lengths, tokens, cotangent, attended, wa, wb, wc.reshape(MLP, D), vec, fb1
     )
     input_grad, grad_lin, sv, sq = back(
-        crop_lengths, vec, vg, tokens, cotangent, wa, wb, wc.reshape(MLP, D), attended, slope, normed_two, normed,
-        projected, lse, grad_fc2
+        crop_lengths, vec, vg, tokens, cotangent, wa, wb, wc.reshape(MLP, D), attended, slope, hidden, normed_two,
+        normed, projected, lse
     )
     moment_one, moment_two, difference, tail, vector_part, norm = adam_step(
         grad_lin, sv, sq, master, first_moment, second_moment
@@ -1489,7 +1501,7 @@
     return (
         block_output,
         input_grad,
-        norm[0, :1],
+        norm.reshape(1),
         vector_part,
         moment_one,
         moment_two,

time: 308 us -> 299 us (0.971)
  Pallas kernels: 300 us -> 293 us
    pallas_call x1, Pallas kernels: 33.1 us -> 23.3 us  [forward(): pl.pallas_call(forward_kernel, name='mlp_forward', out_shape=[S((rows, D)...]
where the time goes in v2:
time: 299 us; the launch traced here: 295 us
  Pallas kernels  293 us (98%)
    pallas_call x1, Pallas kernels, back(): pl.pallas_call(back_kernel, name='back', out_shape=[S((rows, D), F32), S(...  134 us
    pallas_call x1, Pallas kernels, front(): pl.pallas_call(front_kernel, name='front', out_shape=[S((4, D, D), BF16),...  79 us
    pallas_call x1, Pallas kernels, mean_groups(): pl.pallas_call(mean_kernel, name='mean_groups', out_shape=[S((PARTS, 128)...  37.8 us
    pallas_call x1, Pallas kernels, forward(): pl.pallas_call(forward_kernel, name='mlp_forward', out_shape=[S((rows, D)...  23.3 us
    pallas_call x1, Pallas kernels, adam_step(): pl.pallas_call(adam_kernel, name='adam', grid=(BLOCKS + 1,), out_shape=[S...  10.1 us
    pallas_call x1, Pallas kernels, outer_step(): pl.pallas_call(outer_kernel, name='outer', grid=(BLOCKS + 1,), out_shape=...  8.54 us

profile of v2, /device:TPU:0, one launch (start us, length us, event | category | flops | bytes accessed | tf_op | source)
XLA Modules:
  0.0 295.5 jit_solution(10726179970770553405)
XLA Ops:
  0.6 79.0 %front.1 = (bf16[4,768,768]{2,1,0:T(8,128)(2,1)}, bf16[4,768,768]{2,1,0:T(8,128)(2,1)}, bf16[8,4,96,768]{3,2,1,0:T(8,128)(2,1)}, f32[16,768]{1,0:T(8,128)}, f32[...) custom-call(s32[1,10]{1,0:T(1,128)} %lens.5, ...), custom_call_target="tpu_custom_call" | custom-call | tf_op jit(solution)/shard_map/front/pallas_call | solution.py:794
  79.6 23.3 %mlp_forward.1 = (f32[1024,768]{1,0:T(8,128)}, bf16[1024,3072]{1,0:T(8,128)(2,1)}, bf16[1024,768]{1,0:T(8,128)(2,1)}, bf16[1024,3072]{1,0:T(8,128)(2,1)}, f32[16,768]{1,0:T(8,128)}) custom-call(s32[1,10]{1,0:T(1,128)} %lens.5, f32[1024,768]{1,0:T(8,128)} %tok.3, f32[1024,768]{1,0:T(8,128)} %cot.1, bf16[1024,768]{1,0:T(8,128)(2,1)} %get-tuple-element.38.att_in, ...), custom_call_target="tpu_custom_call" | custom-call | tf_op jit(solution)/shard_map/mlp_forward/pallas_call | solution.py:898
  103.0 134.1 %back.1 = (f32[1024,768]{1,0:T(8,128)}, f32[6912,128]{1,0:T(8,128)}, f32[16,128]{1,0:T(8,128)}, f32[8,128]{1,0:T(8,128)}) custom-call(s32[1,10]{1,0:T(1,128)} %lens.5, f32[16,768]{1,0:T(8,128)} %get-tuple-element.42.vec, f32[16,768]{1,0:T(8,128)} %get-tuple-element.45.vg_in, f32[1024,768]{1,0:T(8,128)} %tok.3, f32[1024,768]{1,0:T(8,128)} %cot.1, ...), custom_call_target="tpu_custom_call" | custom-call | tf_op jit(solution)/shard_map/back/pallas_call | solution.py:1245
  237.1 10.1 %adam.1 = (f32[1,886080]{1,0:T(1,128)}, f32[1,886080]{1,0:T(1,128)}, bf16[6912,128]{1,0:T(8,128)(2,1)}, f32[1,1408]{1,0:T(1,128)}, f32[1,1344]{1,0:T(1,128)}, /*index=5*/f32[1,1]{1,0:T(1,128)}) custom-call(f32[6912,128]{1,0:T(8,128)} %get-tuple-element.53.grad, f32[16,128]{1,0:T(8,128)} %get-tuple-element.54.sv, f32[8,128]{1,0:T(8,128)} %get-tuple-element.55.sq, ...), custom_call_target="tpu_custom_call" | custom-call | tf_op jit(solution)/shard_map/adam/pallas_call | solution.py:1335
  247.1 37.8 %mean_groups.1 = (bf16[6912,128]{1,0:T(8,128)(2,1)}, f32[1,1408]{1,0:T(1,128)}) custom-call(bf16[6912,128]{1,0:T(8,128)(2,1)} %get-tuple-element.60.diff, f32[1,1408]{1,0:T(1,128)} %get-tuple-element.61.tail), custom_call_target="tpu_custom_call" | custom-call | tf_op jit(solution)/shard_map/mean_groups/pallas_call | solution.py:1473
  285.0 0.0 copy-start
  285.0 8.5 %outer.1 = (f32[886080]{0:T(1024)}, f32[886080]{0:T(1024)}, f32[886080]{0:T(1024)}) custom-call(bf16[6912,128]{1,0:T(8,128)(2,1)} %get-tuple-element.62.mean, f32[1,1408]{1,0:T(1,128)} %get-tuple-element.63.tail, f32[886080]{0:T(1024)} %master.5, f32[886080]{0:T(1024)} %momentum.1), custom_call_target="tpu_custom_call" | custom-call | tf_op jit(solution)/shard_map/outer/pallas_call | solution.py:1374
  293.5 0.0 copy-done
  293.5 1.7 copy.17
Async XLA Ops:
  285.0 8.5 %copy-start = (f32[1024,768]{1,0:T(8,128)S(1)}, f32[1024,768]{1,0:T(8,128)}, u32[]{:S(2)}) copy-start(f32[1024,768]{1,0:T(8,128)} %get-tuple-element.77) | copy-start | bytes 9437188

commit v3 on v2

--- a/solution.py
+++ b/solution.py
@@ -545,7 +545,7 @@
         value = flat[:, pl.ds(pl.multiple_of(at * 128, 6144), 6144)]
         lin[pl.ds(pl.multiple_of(at, 48), 48), :] = value.reshape(48, 128)
         return 0
-    lax.fori_loop(0, count // 48, body, 0)
+    lax.fori_loop(0, count // 48, body, 0, unroll=8)
 
 
 def weight_strip(w, ref, t):
@@ -561,26 +561,26 @@
 
 
 def front_kernel(
-    lens, master, tok,
+    lens, master, tok_in,
     wa, wb, wc, vec, fb1, normed, proj, att, lse_out,
-    flat, lin, pv, pieces, wv, wa_in, bias, line, column, att_in, lse,
+    tok, early, flat, lin, pv, pieces, wv, wa_in, bias, line, column, att_in, lse,
     ls, zs, zr, xs, xr, ys, yr, ds, dr, cs, cr, vs, vr, es, er,
 ):
+    first_in = pltpu.make_async_copy(master.at[pl.ds(0, 2304 * 128)], early.at[0], ls.at[6])
+    first_in.start()
     weights_in = pltpu.make_async_copy(master, flat.at[0], ls.at[5])
     weights_in.start()
+    tok_load = pltpu.make_async_copy(tok_in, tok, ls.at[7])
+    tok_load.start()
     g, t, z, c, gx, gy = place()
     fulls = (wa, wb, wc)
     peers = [lax.rem(t + k, 8) for k in range(1, 8)]
     barrier = pltpu.get_barrier_semaphore()
     for target in [(g, p) for p in peers] + [(gx, t), (gy, t)]:
         pl.semaphore_signal(barrier, inc=1, device_id=target, device_id_type=MESH_ID)
-    weights_in.wait()
-    to_rows(flat, lin, 0, 2304)
+    first_in.wait()
+    to_rows(early, lin, 0, 2304)
     convert_piece(0, lin, pieces.at[0])
-    pv[...] = jnp.zeros_like(pv)
-    for j in range(14):
-        low = flat[:, pl.ds(6912 * 128 + ROWS * j, ROWS)].astype(BF16)
-        pv[j : j + 1, :ROWS] = low.astype(F32)
     pl.semaphore_wait(barrier, 9)
     other = t + 1 - 2 * c
 
@@ -709,6 +709,11 @@
     own_copy(0).start()
     start_z(0, 0, extra_copy)
     own_local(0).start()
+    weights_in.wait()
+    pv[...] = jnp.zeros_like(pv)
+    for j in range(14):
+        low = flat[:, pl.ds(6912 * 128 + ROWS * j, ROWS)].astype(BF16)
+        pv[j : j + 1, :ROWS] = low.astype(F32)
     local_v = pltpu.make_async_copy(pv, wv.at[t], ls.at[3])
     local_v.start()
     v_copies = [remote(pv, wv.at[t], vs.at[k], vr.at[k], (g, peers[k])) for k in range(7)]
@@ -733,6 +738,7 @@
             fb1[0:1, lead : lead + ROWS] = wv[k, 8 + j : 9 + j, :ROWS]
     arrive(1)
     cross(0)
+    tok_load.wait()
     norm_rows(tok, vec, att)
     move_rows(lambda first, count: to_places(line, first, count), att, normed)
     arrive(2)
@@ -799,9 +805,11 @@
             S((16, D), F32), S((8, MLP), F32),
             S((rows, D), BF16), S((3, rows, D), BF16), S((rows, D), BF16), S((16, rows), F32),
         ],
-        in_specs=[pl.BlockSpec(memory_space=pltpu.SMEM)] + [ANY, vm],
+        in_specs=[pl.BlockSpec(memory_space=pltpu.SMEM)] + [ANY, ANY],
         out_specs=[ANY] * 3 + [vm] * 6,
         scratch_shapes=[
+            pltpu.VMEM((rows, D), F32),
+            pltpu.VMEM((1, 2304 * 128), F32),
             pltpu.VMEM((1, master.shape[0]), F32),
             pltpu.VMEM((6912, 128), F32),
             pltpu.VMEM((16, 128), F32),
@@ -813,7 +821,7 @@
             pltpu.VMEM((rows, 128), jnp.int32),
             pltpu.VMEM((rows, D), BF16),
             pltpu.VMEM((rows, 128), F32),
-            DMA((6,)),
+            DMA((8,)),
             DMA((3, 2, 3)), DMA((3, 2, 3)),
             DMA((3, 2, 3)), DMA((3, 2, 3)),
             DMA((3, 2, 3)), DMA((3, 2, 3)),

time: 299 us -> 298 us (level)
  no operation moved by 1% of the time
where the time goes in v3:
time: 298 us; the launch traced here: 294 us
  Pallas kernels  291 us (98%)
    pallas_call x1, Pallas kernels, back(): pl.pallas_call(back_kernel, name='back', out_shape=[S((rows, D), F32), S(...  134 us
    pallas_call x1, Pallas kernels, front(): pl.pallas_call(front_kernel, name='front', out_shape=[S((4, D, D), BF16),...  77.6 us
    pallas_call x1, Pallas kernels, mean_groups(): pl.pallas_call(mean_kernel, name='mean_groups', out_shape=[S((PARTS, 128)...  37.8 us
    pallas_call x1, Pallas kernels, forward(): pl.pallas_call(forward_kernel, name='mlp_forward', out_shape=[S((rows, D)...  23.3 us
    pallas_call x1, Pallas kernels, adam_step(): pl.pallas_call(adam_kernel, name='adam', grid=(BLOCKS + 1,), out_shape=[S...  10.1 us
    pallas_call x1, Pallas kernels, outer_step(): pl.pallas_call(outer_kernel, name='outer', grid=(BLOCKS + 1,), out_shape=...  8.54 us

profile of v3, /device:TPU:0, one launch (start us, length us, event | category | flops | bytes accessed | tf_op | source)
XLA Modules:
  0.0 294.1 jit_solution(5879029238089967769)
XLA Ops:
  0.6 77.6 %front.1 = (bf16[4,768,768]{2,1,0:T(8,128)(2,1)}, bf16[4,768,768]{2,1,0:T(8,128)(2,1)}, bf16[8,4,96,768]{3,2,1,0:T(8,128)(2,1)}, f32[16,768]{1,0:T(8,128)}, f32[...) custom-call(s32[1,10]{1,0:T(1,128)} %lens.5, ...), custom_call_target="tpu_custom_call" | custom-call | tf_op jit(solution)/shard_map/front/pallas_call | solution.py:800
  78.2 23.3 %mlp_forward.1 = (f32[1024,768]{1,0:T(8,128)}, bf16[1024,3072]{1,0:T(8,128)(2,1)}, bf16[1024,768]{1,0:T(8,128)(2,1)}, bf16[1024,3072]{1,0:T(8,128)(2,1)}, f32[16,768]{1,0:T(8,128)}) custom-call(s32[1,10]{1,0:T(1,128)} %lens.5, f32[1024,768]{1,0:T(8,128)} %tok.1, f32[1024,768]{1,0:T(8,128)} %cot.1, bf16[1024,768]{1,0:T(8,128)(2,1)} %get-tuple-element.38.att_in, ...), custom_call_target="tpu_custom_call" | custom-call | tf_op jit(solution)/shard_map/mlp_forward/pallas_call | solution.py:906
  101.6 134.2 %back.1 = (f32[1024,768]{1,0:T(8,128)}, f32[6912,128]{1,0:T(8,128)}, f32[16,128]{1,0:T(8,128)}, f32[8,128]{1,0:T(8,128)}) custom-call(s32[1,10]{1,0:T(1,128)} %lens.5, f32[16,768]{1,0:T(8,128)} %get-tuple-element.42.vec, f32[16,768]{1,0:T(8,128)} %get-tuple-element.45.vg_in, f32[1024,768]{1,0:T(8,128)} %tok.1, f32[1024,768]{1,0:T(8,128)} %cot.1, ...), custom_call_target="tpu_custom_call" | custom-call | tf_op jit(solution)/shard_map/back/pallas_call | solution.py:1253
  235.7 10.1 %adam.1 = (f32[1,886080]{1,0:T(1,128)}, f32[1,886080]{1,0:T(1,128)}, bf16[6912,128]{1,0:T(8,128)(2,1)}, f32[1,1408]{1,0:T(1,128)}, f32[1,1344]{1,0:T(1,128)}, /*index=5*/f32[1,1]{1,0:T(1,128)}) custom-call(f32[6912,128]{1,0:T(8,128)} %get-tuple-element.53.grad, f32[16,128]{1,0:T(8,128)} %get-tuple-element.54.sv, f32[8,128]{1,0:T(8,128)} %get-tuple-element.55.sq, ...), custom_call_target="tpu_custom_call" | custom-call | tf_op jit(solution)/shard_map/adam/pallas_call | solution.py:1343
  245.8 37.8 %mean_groups.1 = (bf16[6912,128]{1,0:T(8,128)(2,1)}, f32[1,1408]{1,0:T(1,128)}) custom-call(bf16[6912,128]{1,0:T(8,128)(2,1)} %get-tuple-element.60.diff, f32[1,1408]{1,0:T(1,128)} %get-tuple-element.61.tail), custom_call_target="tpu_custom_call" | custom-call | tf_op jit(solution)/shard_map/mean_groups/pallas_call | solution.py:1481
  283.6 0.0 copy-start
  283.6 8.5 %outer.1 = (f32[886080]{0:T(1024)}, f32[886080]{0:T(1024)}, f32[886080]{0:T(1024)}) custom-call(bf16[6912,128]{1,0:T(8,128)(2,1)} %get-tuple-element.62.mean, f32[1,1408]{1,0:T(1,128)} %get-tuple-element.63.tail, f32[886080]{0:T(1024)} %master.5, f32[886080]{0:T(1024)} %momentum.1), custom_call_target="tpu_custom_call" | custom-call | tf_op jit(solution)/shard_map/outer/pallas_call | solution.py:1382
  292.2 0.0 copy-done
  292.2 1.7 copy.17
Async XLA Ops:
  283.6 8.5 %copy-start = (f32[1024,768]{1,0:T(8,128)S(1)}, f32[1024,768]{1,0:T(8,128)}, u32[]{:S(2)}) copy-start(f32[1024,768]{1,0:T(8,128)} %get-tuple-element.77) | copy-start | bytes 9437188

commit v4 on v3

--- a/solution.py
+++ b/solution.py
@@ -1286,7 +1286,7 @@
 SUM_H, SUM_Q, SUM_E = PARTS // 2, PARTS // 4, PARTS // 8
 MATRIX_WIDTH = PARTS * 128
 VECTOR_WIDTH = 14 * ROWS
-BLOCKS = 4
+BLOCKS = 2
 BLOCK = MATRIX_WIDTH // BLOCKS
 CHUNK = 6144
 
@@ -1317,7 +1317,7 @@
             )
             diff[at, :] = ahead.reshape(CHUNK // 128, 128).astype(BF16)
             return 0
-        lax.fori_loop(0, BLOCK // CHUNK, body, 0, unroll=12)
+        lax.fori_loop(0, BLOCK // CHUNK, body, 0, unroll=24)
 
     @pl.when(i == BLOCKS)
     def _():
@@ -1350,6 +1350,7 @@
         in_specs=[rows, whole((16, 128)), whole((8, 128)), pl.BlockSpec((BLOCK,), lambda i: (i,)), line, line],
         out_specs=[line, line, rows, whole((1, 1408)), whole((1, VECTOR_WIDTH)), whole((1, 1))],
         scratch_shapes=[pltpu.VMEM((1, VECTOR_WIDTH), F32)],
+        compiler_params=pltpu.CompilerParams(vmem_limit_bytes=48 * 2**20),
     )(grad, sv, sq, master, first, second)
 
 
@@ -1369,7 +1370,7 @@
             at = pl.ds(pl.multiple_of(n * (CHUNK // 128), CHUNK // 128), CHUNK // 128)
             step(flat, mean[at, :].astype(F32).reshape(CHUNK))
             return 0
-        lax.fori_loop(0, BLOCK // CHUNK, body, 0, unroll=12)
+        lax.fori_loop(0, BLOCK // CHUNK, body, 0, unroll=24)
 
     @pl.when(i == BLOCKS)
     def _():
@@ -1389,6 +1390,7 @@
             pl.BlockSpec((1, 1408), lambda i: (0, 0)), line, line,
         ],
         out_specs=[line] * 3,
+        compiler_params=pltpu.CompilerParams(vmem_limit_bytes=48 * 2**20),
     )(mean, tail, master, momentum)
 
 

time: 298 us -> 301 us (1.010)
  local copies, waits for them, and re-layouts: 1.67 us -> 8.99 us
  Pallas kernels: 291 us -> 287 us
    unnamed x3 -> x19, local copies, waits for them, and re-layouts: 1.67 us -> 8.99 us
where the time goes in v4:
time: 301 us; the launch traced here: 297 us
  Pallas kernels  287 us (95%)
  local copies, waits for them, and re-layouts  8.99 us (3%)
    pallas_call x1, Pallas kernels, back(): pl.pallas_call(back_kernel, name='back', out_shape=[S((rows, D), F32), S(...  134 us
    pallas_call x1, Pallas kernels, front(): pl.pallas_call(front_kernel, name='front', out_shape=[S((4, D, D), BF16),...  77.6 us
    pallas_call x1, Pallas kernels, mean_groups(): pl.pallas_call(mean_kernel, name='mean_groups', out_shape=[S((PARTS, 128)...  37.8 us
    pallas_call x1, Pallas kernels, forward(): pl.pallas_call(forward_kernel, name='mlp_forward', out_shape=[S((rows, D)...  23.3 us
    unnamed x19, local copies, waits for them, and re-layouts  8.99 us
    pallas_call x1, Pallas kernels, adam_step(): pl.pallas_call(adam_kernel, name='adam', grid=(BLOCKS + 1,), out_shape=[S...  8.04 us
    pallas_call x1, Pallas kernels, outer_step(): pl.pallas_call(outer_kernel, name='outer', grid=(BLOCKS + 1,), out_shape=...  6.38 us

profile of v4, /device:TPU:0, one launch (start us, length us, event | category | flops | bytes accessed | tf_op | source)
XLA Modules:
  0.0 297.3 jit_solution(12743334124236103226)
XLA Ops:
  0.6 77.6 %front.1 = (bf16[4,768,768]{2,1,0:T(8,128)(2,1)}, bf16[4,768,768]{2,1,0:T(8,128)(2,1)}, bf16[8,4,96,768]{3,2,1,0:T(8,128)(2,1)}, f32[16,768]{1,0:T(8,128)}, f32[...) custom-call(s32[1,10]{1,0:T(1,128)} %lens.5, ...), custom_call_target="tpu_custom_call" | custom-call | tf_op jit(solution)/shard_map/front/pallas_call | solution.py:800
  78.2 23.3 %mlp_forward.1 = (f32[1024,768]{1,0:T(8,128)}, bf16[1024,3072]{1,0:T(8,128)(2,1)}, bf16[1024,768]{1,0:T(8,128)(2,1)}, bf16[1024,3072]{1,0:T(8,128)(2,1)}, f32[16,768]{1,0:T(8,128)}) custom-call(s32[1,10]{1,0:T(1,128)} %lens.5, f32[1024,768]{1,0:T(8,128)} %tok.1, f32[1024,768]{1,0:T(8,128)} %cot.1, bf16[1024,768]{1,0:T(8,128)(2,1)} %get-tuple-element.38.att_in, ...), custom_call_target="tpu_custom_call" | custom-call | tf_op jit(solution)/shard_map/mlp_forward/pallas_call | solution.py:906
  101.6 134.2 %back.1 = (f32[1024,768]{1,0:T(8,128)}, f32[6912,128]{1,0:T(8,128)}, f32[16,128]{1,0:T(8,128)}, f32[8,128]{1,0:T(8,128)}) custom-call(s32[1,10]{1,0:T(1,128)} %lens.5, f32[16,768]{1,0:T(8,128)} %get-tuple-element.42.vec, f32[16,768]{1,0:T(8,128)} %get-tuple-element.45.vg_in, f32[1024,768]{1,0:T(8,128)} %tok.1, f32[1024,768]{1,0:T(8,128)} %cot.1, ...), custom_call_target="tpu_custom_call" | custom-call | tf_op jit(solution)/shard_map/back/pallas_call | solution.py:1253
  235.8 0.0 copy-start.1
  235.8 2.0 copy-done.1
  237.8 0.0 copy-start.4
  237.8 0.7 copy-done.4
  238.5 0.0 copy-start.7
  238.5 0.7 copy-done.7
  239.1 0.0 copy-start
  239.1 8.0 %adam.1 = (f32[1,886080]{1,0:T(1,128)}, f32[1,886080]{1,0:T(1,128)}, bf16[6912,128]{1,0:T(8,128)(2,1)S(1)}, f32[1,1408]{1,0:T(1,128)S(1)}, f32[1,1344]{1,0:T(1,128)}, /*index=5*/f32[1,1]{1,0:T(1,128)}) custom-call(f32[6912,128]{1,0:T(8,128)S(1)} %copy-done.1, f32[16,128]{1,0:T(8,128)S(1)} %copy-done.4, f32[8,128]{1,0:T(8,128)S(1)} %copy-done.7, ...), custom_call_target="tpu_custom_call" | custom-call | tf_op jit(solution)/shard_map/adam/pallas_call | solution.py:1343
  247.2 0.0 copy-start.2
  247.2 1.2 copy-done.2
  248.4 0.0 copy-start.5
  248.4 0.6 copy-done.5
  249.0 37.8 %mean_groups.1 = (bf16[6912,128]{1,0:T(8,128)(2,1)}, f32[1,1408]{1,0:T(1,128)}) custom-call(bf16[6912,128]{1,0:T(8,128)(2,1)} %copy-done.2, f32[1,1408]{1,0:T(1,128)} %copy-done.5), custom_call_target="tpu_custom_call" | custom-call | tf_op jit(solution)/shard_map/mean_groups/pallas_call | solution.py:1483
  286.8 0.0 copy-done
  286.8 0.0 copy-start.3
  286.8 1.5 copy-done.3
  288.3 0.0 copy-start.6
  288.3 0.7 copy-done.6
  289.0 0.0 copy-start.8
  289.0 6.4 %outer.1 = (f32[886080]{0:T(1024)}, f32[886080]{0:T(1024)}, f32[886080]{0:T(1024)}) custom-call(bf16[6912,128]{1,0:T(8,128)(2,1)S(1)} %copy-done.3, f32[1,1408]{1,0:T(1,128)S(1)} %copy-done.6, f32[886080]{0:T(1024)S(1)} %copy-done, f32[886080]{0:T(1024)} %momentum.1), custom_call_target="tpu_custom_call" | custom-call | tf_op jit(solution)/shard_map/outer/pallas_call | solution.py:1383
  295.4 0.0 copy-done.8
  295.4 1.7 copy.17
Async XLA Ops:
  235.8 2.0 copy-start.1
  237.8 0.7 copy-start.4
  238.5 0.7 copy-start.7
  239.1 47.7 %copy-start = (f32[886080]{0:T(1024)S(1)}, f32[886080]{0:T(1024)}, u32[]{:S(2)}) copy-start(f32[886080]{0:T(1024)} %master.5) | copy-start | bytes 10632964
  247.2 1.2 copy-start.2
  248.4 0.6 copy-start.5
  286.8 1.5 copy-start.3
  288.3 0.7 copy-start.6
  289.0 6.4 %copy-start.8 = (f32[1024,768]{1,0:T(8,128)S(1)}, f32[1024,768]{1,0:T(8,128)}, u32[]{:S(2)}) copy-start(f32[1024,768]{1,0:T(8,128)} %get-tuple-element.77) | copy-start | bytes 9437188
